TPU v7x, 512 devices: a whole 4x4x16 slice. The times are simulated.
512 devices in a mesh: ctx: 32 (over z, core), tp: 16 (over x, y).
Axes of the slice: x: 4, y: 4, z: 16, core: 2. Of those that a mesh axis runs over, the one named last changes fastest.
Arguments:
- hidden: bfloat16 [32768, 6144], P('ctx', 'tp'), may hold values from -6 to 6
- base_query_key_value: bfloat16 [3, 32768, 8192], P(None, 'ctx', 'tp'), may hold values from -54 to 54
- adapter_down_weight: bfloat16 [6144, 64], P('tp'), may hold values from -0.078125 to 0.078125
- adapter_up_weight: bfloat16 [3, 64, 8192], P(None, None, 'tp'), may hold values from -0.75 to 0.75
- token_log_decay: float32 [32768, 64], P('ctx', 'tp'), may hold values from -2.3 to 0, as said below
- output_norm_gain: float32 [8192], P('tp'), may hold values from 0.25 to 1.75
Outputs:
- mixed_out: bfloat16 [32768, 8192], P('ctx', 'tp')
- block_states: float32 [32, 64, 128, 128], P('ctx', 'tp')
Inputs may be any that keep to these rules, and one draw needn't show every extreme that they name: `token_log_decay`: every entry is negative.
All inputs are finite; a program needn't handle non-finite values.
Results may differ from a plain program's by a relative error of at most 0.023.
Values may be sent and summed in bfloat16 or wider, within the bound.
A program may use at most 64 MiB of HBM per device.

v0:
```python
import jax
import jax.numpy as jnp
from jax import lax
from jax.sharding import PartitionSpec as P

HD = 128


def prefix(x, axis, combine, identity):
    peers, here = (lax.axis_size(axis), lax.axis_index(axis))
    everything = jax.tree.map(
        lambda part, kind: lax.all_gather(part.astype(kind), axis), x, (jnp.bfloat16, jnp.bfloat16)
    )
    start = jax.tree.map(
        lambda part, zero: jnp.broadcast_to(jnp.asarray(zero, part.dtype), part.shape), x, identity
    )

    def hop(k, before):
        reached = k < here
        new = combine(
            before, jax.tree.map(lambda part, own: part[k].astype(own.dtype), everything, x)
        )
        return jax.tree.map(lambda a, b: jnp.where(reached, a, b), new, before)

    return lax.fori_loop(0, peers, hop, start)


def local(
    hidden,
    base_query_key_value,
    adapter_down_weight,
    adapter_up_weight,
    token_log_decay,
    output_norm_gain,
):
    tok_count = hidden.shape[0]
    head_number_total = token_log_decay.shape[1]
    partial_output_rows = jnp.dot(hidden, adapter_down_weight, preferred_element_type=jnp.float32)
    adapter_row_values = lax.psum(partial_output_rows.astype(jnp.bfloat16), "tp")
    projected_rows = base_query_key_value.astype(jnp.float32) + jnp.einsum(
        "uz,ozh->ouh", adapter_row_values, adapter_up_weight, preferred_element_type=jnp.float32
    )
    query = jax.nn.silu(projected_rows[0]).astype(jnp.bfloat16)
    key_rows = jax.nn.silu(projected_rows[1]).astype(jnp.bfloat16)
    value = projected_rows[2].astype(jnp.bfloat16)
    cumulative = jnp.cumsum(token_log_decay, axis=0)
    last_sum = cumulative[-1]
    key_heads = key_rows.reshape(tok_count, head_number_total, HD)
    value_head_rows = value.reshape(tok_count, head_number_total, HD)
    query_heads = query.reshape(tok_count, head_number_total, HD)
    key_scaled = (
        key_heads.astype(jnp.float32) * jnp.exp(last_sum[None, :] - cumulative)[:, :, None]
    ).astype(jnp.bfloat16)
    local_state = jnp.einsum(
        "shd,she->hde", key_scaled, value_head_rows, preferred_element_type=jnp.float32
    )
    block_decay = jnp.exp(last_sum)

    def combine(preceding_blocks, latter):
        return (
            preceding_blocks[0] * latter[0],
            latter[0][:, None, None] * preceding_blocks[1] + latter[1],
        )

    identity = (jnp.ones_like(block_decay), jnp.zeros_like(local_state))
    decay_before, prior_state = prefix((block_decay, local_state), "ctx", combine, identity)
    state_out = block_decay[:, None, None] * prior_state + local_state
    carried = prior_state.astype(jnp.bfloat16)
    earlier_part = (
        jnp.einsum("thd,hde->the", query_heads, carried, preferred_element_type=jnp.float32)
        * jnp.exp(cumulative)[:, :, None]
    )
    causal = jnp.arange(tok_count)[:, None] >= jnp.arange(tok_count)[None, :]

    def one_head(head_index):
        query_head = lax.dynamic_slice_in_dim(query, head_index * HD, HD, 1)
        key_head = lax.dynamic_slice_in_dim(key_rows, head_index * HD, HD, 1)
        value_head = lax.dynamic_slice_in_dim(value, head_index * HD, HD, 1)
        cumulative_head = lax.dynamic_index_in_dim(cumulative, head_index, 1, keepdims=False)
        scores = lax.dot_general(
            query_head, key_head, (((1,), (1,)), ((), ())), preferred_element_type=jnp.float32
        )
        spread = cumulative_head[:, None] - cumulative_head[None, :]
        decayed = jnp.exp(jnp.where(causal, spread, 0.0))
        weights = jnp.where(causal, decayed * scores, 0.0).astype(jnp.bfloat16)
        return jnp.dot(weights, value_head, preferred_element_type=jnp.float32)

    inside = jnp.moveaxis(lax.map(one_head, jnp.arange(head_number_total, dtype=jnp.int32)), 0, 1)
    attended = inside + earlier_part
    mean_square = jnp.mean(attended * attended, axis=-1, keepdims=True)
    normed = (
        attended
        * lax.rsqrt(mean_square + 1e-06)
        * output_norm_gain.reshape(head_number_total, HD)[None]
    )
    mixed_out = normed.reshape(tok_count, head_number_total * HD).astype(jnp.bfloat16)
    return (mixed_out, state_out[None])


def solution(mesh):
    in_specs = (
        P("ctx", "tp"),
        P(None, "ctx", "tp"),
        P("tp", None),
        P(None, None, "tp"),
        P("ctx", "tp"),
        P("tp"),
    )
    out_specs = (P("ctx", "tp"), P("ctx", "tp", None, None))
    return jax.shard_map(local, mesh=mesh, in_specs=in_specs, out_specs=out_specs, check_vma=False)
```

profile of v0, /device:TPU:1, one launch (start us, length us, event | category | flops | bytes accessed | tf_op | source)
XLA Modules:
  0.0 263.7 jit_solution(15598879978430241254)
XLA Ops:
  7.2 1.1 copy-done
  8.3 1.8 convolution_convert_fusion
  10.2 0.7 copy.73
  10.9 1.1 reduce-window.6
  12.7 4.7 %copy.38 = bf16[3,1024,512]{1,2,0:T(8,128)(2,1)} copy(bf16[3,1024,512]{2,1,0:T(8,128)(2,1)} %param.11) | data formatting | bytes 6291456 | tf_op args[1]
  17.5 111.1 %all-reduce.2.cloned.1.call-done = bf16[1024,64]{0,1:T(8,128)(2,1)} async-done(((bf16[1024,64]{0,1:T(8,128)(2,1)}), bf16[1024,64]{0,1:T(8,128)(2,1)}) %all-reduce.2.cloned.1.call-update) | async-done | bytes 131088 | tf_op jit(solution)/shard_map/psum | solution.py:39
  128.6 3.0 %bitcast_add_fusion = f32[3,1024,512]{1,2,0:T(8,128)S(1)} fusion(bf16[3,1024,512]{1,2,0:T(8,128)(2,1)} %copy.38, bf16[3,64,512]{2,1,0:T(8,128)(2,1)S(1)} %copy-done.3, bf16[1024,64]{0,1:T(8,128)(2,1)} %all-reduce.2.cloned.1.call-done), kind=kOutput, calls=%fused_computation.19 | convolution fusion | flops 204472320 | bytes 9764864 | tf_op jit(solution)/shard_map/uz,ozh->ouh/dot_general | solution.py:40
  131.6 2.1 fusion.36
  133.7 1.2 copy-done.1
  134.9 1.1 slice.37
  136.0 3.0 %copy.45 = f32[1024,4,128]{2,0,1:T(8,128)} copy(f32[1024,4,128]{0,2,1:T(8,128)} %bitcast.99) | data formatting | bytes 4194304 | tf_op jit(solution)/shard_map/squeeze | solution.py:44
  139.0 3.9 %fusion.37 = (bf16[4,128,128]{2,1,0:T(8,128)(2,1)}, f32[4,128,128]{2,1,0:T(8,128)S(1)}) fusion(bf16[1024,4,128]{0,2,1:T(8,128)(2,1)} %bitcast.101, f32[1024,4]{0,1:T(4,128)S(1)} %get-tuple-element.267, f32[1024,4,128]{2,0,1:T(8,128)} %copy.45), kind=kOutput, calls=%fused_computation.59 | convolution fusion | flops 138477568 | bytes 3555328 | tf_op jit(solution)/shard_map/shd,she->hde/dot_general | solution.py:54
  142.9 0.2 fusion.32
  143.1 32.9 %all-gather.1 = bf16[32,1,4]{2,1,0:T(2,128)(2,1)S(1)} all-gather(bf16[1,1,4]{2,1,0:T(2,128)(2,1)S(1)} %bitcast.111), channel_id=1, replica_groups=mesh['ctx'=32,'tp'=16] {'ctx'}, dimensions={0}, use_global_device_ids=true | all-gather | bytes 264 | tf_op jit(solution)/shard_map/all_gather | solution.py:12
  176.1 1.8 copy.50
  177.9 2.8 %slice_bitcast_fusion = bf16[1024,512]{0,1:T(8,128)(2,1)} fusion(f32[3,1024,512]{1,2,0:T(8,128)} %copy-done.1), kind=kLoop, calls=%fused_computation.60 | loop fusion | bytes 2097152 | tf_op jit(solution)/shard_map/convert_element_type | solution.py:45
  180.7 4.7 %fusion.27 = (bf16[1024,512]{0,1:T(8,128)(2,1)}, bf16[1024,512]{0,1:T(8,128)(2,1)}) fusion(f32[3,1024,512]{1,2,0:T(8,128)} %copy-done.1), kind=kLoop, calls=%fused_computation.39 | loop fusion | flops 5242880 | bytes 6291456 | tf_op jit(solution)/shard_map/convert_element_type | solution.py:44
  185.4 26.3 %while.26 = (s32[]{:T(128)}, f32[4,1024,128]{1,2,0:T(8,128)}, s32[4]{0:T(128)S(1)}, f32[1024,4]{0,1:T(4,128)S(1)}, bf16[1024,512]{0,1:T(8,128)(2,1)}, /*index=5*...) while((s32[]{:T(128)}, f32[4,1024,128]{1,2,0:T(8,128)}, ...), condition=%wide.region_4.5_spmd.clone.clone, body=%wide.region_3.4_spmd.clone.clone.sunk | while | flops 543162368 | bytes 1329365 | solution.py:88
  185.4 0.7 dynamic_slice.65
  188.9 3.1 %fusion.50 = f32[4,1024,128]{1,2,0:T(8,128)} fusion(f32[4,1024,128]{1,2,0:T(8,128)} %get-tuple-element.381, s32[]{:T(128)} %get-tuple-element.380, f32[1024]{0:T(1024)S(1)} %bitcast.106, bf16[1024,512]{0,1:T(8,128)(2,1)} %get-tuple-element.398, s32[]{:T(128)S(6)} %select_n.81, bf16[1024,512]{0,1:T(8,128)(2,1)} %get-tuple-element.397, ...), kind=kOutput, calls=%fused_computation.9.clone.1 | convolution fusion | flops 543162368 | bytes 1320960 | tf_op jit(solution)/shard_map/while/body/eval_jaxpr/dot_general | solution.py:86
  192.0 0.7 dynamic_slice.65
  195.5 3.2 %fusion.50 = f32[4,1024,128]{1,2,0:T(8,128)} fusion(f32[4,1024,128]{1,2,0:T(8,128)} %get-tuple-element.381, s32[]{:T(128)} %get-tuple-element.380, f32[1024]{0:T(1024)S(1)} %bitcast.106, bf16[1024,512]{0,1:T(8,128)(2,1)} %get-tuple-element.398, s32[]{:T(128)S(6)} %select_n.81, bf16[1024,512]{0,1:T(8,128)(2,1)} %get-tuple-element.397, ...), kind=kOutput, calls=%fused_computation.9.clone.1 | convolution fusion | flops 543162368 | bytes 1320960 | tf_op jit(solution)/shard_map/while/body/eval_jaxpr/dot_general | solution.py:86
  198.7 0.7 dynamic_slice.65
  202.1 3.1 %fusion.50 = f32[4,1024,128]{1,2,0:T(8,128)} fusion(f32[4,1024,128]{1,2,0:T(8,128)} %get-tuple-element.381, s32[]{:T(128)} %get-tuple-element.380, f32[1024]{0:T(1024)S(1)} %bitcast.106, bf16[1024,512]{0,1:T(8,128)(2,1)} %get-tuple-element.398, s32[]{:T(128)S(6)} %select_n.81, bf16[1024,512]{0,1:T(8,128)(2,1)} %get-tuple-element.397, ...), kind=kOutput, calls=%fused_computation.9.clone.1 | convolution fusion | flops 543162368 | bytes 1320960 | tf_op jit(solution)/shard_map/while/body/eval_jaxpr/dot_general | solution.py:86
  205.2 0.7 dynamic_slice.65
  208.7 3.1 %fusion.50 = f32[4,1024,128]{1,2,0:T(8,128)} fusion(f32[4,1024,128]{1,2,0:T(8,128)} %get-tuple-element.381, s32[]{:T(128)} %get-tuple-element.380, f32[1024]{0:T(1024)S(1)} %bitcast.106, bf16[1024,512]{0,1:T(8,128)(2,1)} %get-tuple-element.398, s32[]{:T(128)S(6)} %select_n.81, bf16[1024,512]{0,1:T(8,128)(2,1)} %get-tuple-element.397, ...), kind=kOutput, calls=%fused_computation.9.clone.1 | convolution fusion | flops 543162368 | bytes 1320960 | tf_op jit(solution)/shard_map/while/body/eval_jaxpr/dot_general | solution.py:86
  211.8 6.4 %all-gather.4.cloned.1.call-done = bf16[128,128,128]{2,1,0:T(8,128)(2,1)} async-done(((bf16[4,128,128]{2,1,0:T(8,128)(2,1)}), bf16[128,128,128]{2,1,0:T(8,128)(2,1)}) %all-gather.4.cloned.1.call-update) | async-done | bytes 4194320 | tf_op jit(solution)/shard_map/all_gather | solution.py:12
  218.2 33.7 %while.27 = (s32[]{:T(128)}, f32[4,128,128]{2,1,0:T(8,128)S(1)}, s32[]{:T(128)}, bf16[32,4]{1,0:T(8,128)(2,1)S(1)}, bf16[32,4,128,128]{3,2,1,0:T(8,128)(2,1)}, /*index=5*/s32[]{:T(128)}, s32[]{:T(128)}) while((s32[]{:T(128)}, f32[4,128,128]{2,1,0:T(8,128)S(1)}, s32[]{:T(128)}, bf16[32,4]{1,0:T(8,128)(2,1)S(1)}, ...), condition=%wide.region_6.7_spmd.clone, body=%wide.region_5.6_spmd.clone.sunk | while | flops 327688 | bytes 655505 | solution.py:25
  218.2 1.0 fusion.51
  219.3 1.0 fusion.51
  220.3 1.0 fusion.51
  221.4 1.0 fusion.51
  222.4 1.0 fusion.51
  223.5 1.0 fusion.51
  224.5 1.0 fusion.51
  225.6 1.0 fusion.51
  226.6 1.0 fusion.51
  227.7 1.0 fusion.51
  228.8 1.0 fusion.51
  229.8 1.0 fusion.51
  230.9 1.0 fusion.51
  231.9 1.0 fusion.51
  233.0 1.0 fusion.51
  234.0 1.0 fusion.51
  235.1 1.0 fusion.51
  236.1 1.0 fusion.51
  237.2 1.0 fusion.51
  238.2 1.0 fusion.51
  239.3 1.0 fusion.51
  240.3 1.0 fusion.51
  241.4 1.0 fusion.51
  242.5 1.0 fusion.51
  243.5 1.0 fusion.51
  244.6 1.0 fusion.51
  245.6 1.0 fusion.51
  246.7 1.0 fusion.51
  247.7 1.0 fusion.51
  248.8 1.0 fusion.51
  249.8 1.0 fusion.51
  250.9 1.0 fusion.51
  251.9 2.5 multiply_reduce_fusion
  254.5 0.3 multiply_convert_fusion
  254.7 1.3 copy.52
  256.1 0.8 add_bitcast_fusion
  (61 shorter events, 1.4 us)
Async XLA Ops:
  7.2 1.1 copy-start
  7.2 121.4 %all-reduce.2.cloned.1.call-start = ((), (), s32[]{:S(2)}) async-start(), calls=%async_computation | async-start | bytes 262144 | tf_op jit(solution)/shard_map/psum | solution.py:39
  10.2 208.1 %all-gather.4.cloned.1.call-start = ((), (), s32[]{:S(2)}) async-start(), calls=%async_computation.1 | async-start | bytes 4325376 | tf_op jit(solution)/shard_map/all_gather | solution.py:12
  12.7 115.9 %copy-start.3 = (bf16[3,64,512]{2,1,0:T(8,128)(2,1)S(1)}, bf16[3,64,512]{2,1,0:T(8,128)(2,1)}, u32[]{:S(2)}) copy-start(bf16[3,64,512]{2,1,0:T(8,128)(2,1)} %param.13) | copy-start | bytes 589828
  131.6 3.3 %copy-start.1 = (f32[3,1024,512]{1,2,0:T(8,128)}, f32[3,1024,512]{1,2,0:T(8,128)S(1)}, u32[]{:S(2)}) copy-start(f32[3,1024,512]{1,2,0:T(8,128)S(1)} %bitcast_add_fusion) | copy-start | bytes 18874372
  185.4 66.5 %copy-start.2 = (f32[1024,4,128]{2,0,1:T(8,128)S(1)}, f32[1024,4,128]{2,0,1:T(8,128)}, u32[]{:S(2)}) copy-start(f32[1024,4,128]{2,0,1:T(8,128)} %copy.50) | copy-start | bytes 6291460
  251.9 2.6 copy-start.4
Sparse Core Ops, SparseCore 0:
  11.8 116.7 all-reduce.1
  143.0 75.2 all-gather.3
where the time goes:
time: 265 us; the launch traced here: 264 us
  waiting for transfers between devices  118 us (45%)
  other arithmetic  40.2 us (15%)
  blocking collectives  32.9 us (12%)
  matrix products  23.7 us (9%)
  local copies, waits for them, and re-layouts  23.1 us (9%)
  between operations  14.2 us (5%)
  loops' own time  12.1 us (5%)
    psum x1, waiting for transfers between devices, local(): lax.psum(partial_output_rows.astype(jnp.bfloat16), 'tp')  111 us
    all_gather x1, blocking collectives, prefix(): lax.all_gather(part.astype(kind), axis)  32.9 us
    select_n x32, other arithmetic, hop(): return jax.tree.map(lambda a, b: jnp.where(reached, a, b), new, before)  32.4 us
    dot_general x4, matrix products, one_head(): return jnp.dot(weights, value_head, preferred_element_type=jnp.float32)  12.5 us
    another operation x1, loops' own time, local(): lax.map(one_head, jnp.arange(head_number_total, dtype=jnp.int32))  11.1 us
    unnamed x15, local copies, waits for them, and re-layouts  9.15 us
    all_gather x1, waiting for transfers between devices, prefix(): lax.all_gather(part.astype(kind), axis)  6.43 us
  transfers between devices with their start and end apart: 2, of which 2 were waited for; matrix products, arithmetic and copies ran while one was open for 12% of the time, Pallas kernels for 0%

commit v1 on v0

v1 whole, which is shorter than its diff:
```python
import jax
import jax.numpy as jnp
from jax import lax
from jax.experimental import pallas as pl
from jax.experimental.pallas import tpu as pltpu
from jax.sharding import PartitionSpec as P

HD = 128
HEADS = 4
TOK = 1024
HALF = 512
RANK = 64
GROUP = 384
WIDTH = HEADS * HD
PAIR = 2 * HD
BLK = 256
NX, NY, NZ = 4, 4, 16
NTP = NX * NY
LORA_PIECE = HALF // NTP
STATE_PIECE = PAIR // NZ
MESH = pl.DeviceIdType.MESH
F32, BF16 = jnp.float32, jnp.bfloat16


def ring(offset, size):
    return min(offset, size - offset)


XY = sorted(range(1, NTP), key=lambda r: -(ring(r // NY, NX) + ring(r % NY, NY)))
ZZ = sorted(range(1, NZ), key=lambda r: -ring(r, NZ))


def silu(v):
    half = 0.5 * v
    return half + half * jnp.tanh(half)


def kernel(
    hid_hbm, base_hbm, dwn_hbm, up_hbm, dec_hbm, gain_hbm,
    out_hbm, st_hbm,
    hid, base, dpad, upad, dec, gain,
    part, rsum, lora,
    cum, wgt, ccol, dl_own, dl_peer, dl_chip,
    q_ref, qs_ref, kt_ref, v_ref, inside, out_v,
    loc, loc_send, loc_recv, tot, p1, pre, c2, carried, st_v,
    in_sem, out_sem, st_sem,
    rs_s, rs_r, ag_s, ag_r, zs_s, zs_r, zg_s, zg_r, dz_s, dz_r, core_s, core_r,
):
    ctx, tp = lax.axis_index("ctx"), lax.axis_index("tp")
    z, c = ctx // 2, ctx % 2
    x, y = tp // NY, tp % NY
    peer = {"ctx": z * 2 + (1 - c)}

    def plane(r):
        return {"tp": lax.rem(x + r // NY, NX) * NY + lax.rem(y + r % NY, NY)}

    def along(r):
        return {"ctx": lax.rem(z + r, NZ) * 2 + c}

    barrier = pltpu.get_barrier_semaphore()
    for r in ZZ:
        pl.semaphore_signal(barrier, inc=1, device_id=along(r), device_id_type=MESH)
    for r in XY:
        pl.semaphore_signal(barrier, inc=1, device_id=plane(r), device_id_type=MESH)
    pl.semaphore_signal(barrier, inc=1, device_id=peer, device_id_type=MESH)

    loads = [
        pltpu.make_async_copy(dwn_hbm, dpad.at[pl.ds(RANK, RANK)], in_sem.at[0]),
        pltpu.make_async_copy(hid_hbm, hid, in_sem.at[1]),
        pltpu.make_async_copy(dec_hbm, dec, in_sem.at[2]),
        pltpu.make_async_copy(up_hbm, upad.at[:, pl.ds(RANK, RANK)], in_sem.at[3]),
        pltpu.make_async_copy(base_hbm, base, in_sem.at[4]),
        pltpu.make_async_copy(gain_hbm, gain, in_sem.at[5]),
    ]
    for load in loads:
        load.start()

    zeros = jnp.zeros((RANK, GROUP), BF16)
    dpad[pl.ds(0, RANK), :] = zeros
    dpad[pl.ds(2 * RANK, RANK), :] = zeros
    zeros = jnp.zeros((RANK, WIDTH), BF16)
    for i in range(3):
        upad[i, pl.ds(0, RANK), :] = zeros
        upad[i, pl.ds(2 * RANK, RANK), :] = zeros

    loads[0].wait()
    loads[1].wait()
    trans_b = (((1,), (1,)), ((), ()))
    for i in range(2):
        rows = pl.ds(i * BLK, BLK)
        mine = lax.dot_general(
            hid[rows, :], dpad[pl.ds(RANK, 2 * RANK), :], trans_b, preferred_element_type=F32
        ) + lax.dot_general(
            hid[pl.ds(HALF + i * BLK, BLK), :], dpad[pl.ds(0, 2 * RANK), :], trans_b,
            preferred_element_type=F32,
        )
        part[rows, :] = mine.astype(BF16)

    pl.semaphore_wait(barrier, NTP - 1 + NZ - 1 + 1)

    def rs(r):
        to = plane(r)
        return pltpu.make_async_remote_copy(
            part.at[pl.ds(pl.multiple_of(to["tp"] * LORA_PIECE, LORA_PIECE), LORA_PIECE)],
            rsum.at[r], rs_s.at[r], rs_r.at[r], device_id=to, device_id_type=MESH,
        )

    for r in XY:
        rs(r).start()

    loads[2].wait()
    run = jnp.concatenate([dec[...], jnp.zeros((8 - HEADS, TOK), F32)], axis=0)
    lane = lax.broadcasted_iota(jnp.int32, (8, TOK), 1)
    step = 1
    while step < TOK:
        run = run + jnp.where(lane >= step, pltpu.roll(run, step, 1), 0.0)
        step *= 2
    last = run[:, TOK - 1 :]
    cum[...] = run
    wgt[...] = jnp.exp(last - run)
    dl_own[...] = jnp.broadcast_to(last, (8, HD))
    swap_decay = pltpu.make_async_remote_copy(
        dl_own, dl_peer, core_s.at[0], core_r.at[0], device_id=peer, device_id_type=MESH
    )
    swap_decay.start()

    def ccol_of(h, carry):
        ccol[h] = jnp.broadcast_to(cum[pl.ds(h, 1), :], (HD, TOK)).T
        return carry

    lax.fori_loop(0, HEADS, ccol_of, 0)

    swap_decay.wait()
    dl_chip[z] = dl_own[...] + dl_peer[...]

    def dz(r):
        return pltpu.make_async_remote_copy(
            dl_chip.at[z], dl_chip.at[z], dz_s.at[r], dz_r.at[r],
            device_id=along(r), device_id_type=MESH,
        )

    for r in ZZ:
        dz(r).start()

    mine_at = pl.ds(pl.multiple_of(tp * LORA_PIECE, LORA_PIECE), LORA_PIECE)
    for r in XY:
        rs(r).wait_recv()
    total = part[mine_at, :].astype(F32)
    for r in range(1, NTP):
        total = total + rsum[r].astype(F32)
    lora[mine_at, :] = total.astype(BF16)

    def ag(r):
        return pltpu.make_async_remote_copy(
            lora.at[mine_at], lora.at[mine_at], ag_s.at[r], ag_r.at[r],
            device_id=plane(r), device_id_type=MESH,
        )

    for r in XY:
        ag(r).start()
    for r in XY:
        rs(r).wait_send()
    for r in ZZ:
        dz(r).wait()
    loads[3].wait()
    loads[4].wait()
    loads[5].wait()
    for r in XY:
        ag(r).wait_recv()

    def projected(i, a, row, lanes):
        return base[i, pl.ds(a * HALF + row, BLK), lanes].astype(F32) + jnp.dot(
            lora[pl.ds(row, BLK), :],
            upad[i, pl.ds(RANK - RANK * a, 2 * RANK), lanes],
            preferred_element_type=F32,
        )

    def keys_values(pair):
        lanes = pl.ds(pl.multiple_of(pair * PAIR, PAIR), PAIR)
        for a in range(2):
            for row in range(0, HALF, BLK):
                rows = pl.ds(a * HALF + row, BLK)
                k = silu(projected(1, a, row, lanes)).astype(BF16)
                kt_ref[lanes, rows] = k.T
                v_ref[rows, lanes] = projected(2, a, row, lanes).astype(BF16)
        for e in range(2):
            h = pair * 2 + e
            at = pl.ds(pl.multiple_of(h * HD, HD), HD)
            scaled = (kt_ref[at, :].astype(F32) * wgt[pl.ds(h, 1), :]).astype(BF16)
            loc[at, :] = jnp.dot(scaled, v_ref[:, at], preferred_element_type=F32)

    ours = pl.ds(pl.multiple_of(c * PAIR, PAIR), PAIR)
    theirs = pl.ds(pl.multiple_of((1 - c) * PAIR, PAIR), PAIR)
    even = c == 0

    keys_values(1 - c)
    loc_send[...] = loc[theirs, :].astype(BF16)
    swap_local = pltpu.make_async_remote_copy(
        loc_send, loc_recv, core_s.at[1], core_r.at[1], device_id=peer, device_id_type=MESH
    )
    swap_local.start()
    keys_values(c)
    swap_local.wait()

    def per_row(ref, e):
        return jnp.exp(ref[pl.ds(c * 2 + e, 1), :])

    for e in range(2):
        rows = pl.ds(e * HD, HD)
        own = loc[pl.ds(pl.multiple_of(c * PAIR + e * HD, HD), HD), :]
        other = loc_recv[rows, :].astype(F32)
        odd_decay = jnp.where(even, per_row(dl_peer, e), per_row(dl_own, e))
        tot[rows, :] = (
            jnp.where(even, own, other) * odd_decay + jnp.where(even, other, own)
        ).astype(BF16)

    def zs(r):
        to = along(r)
        there = lax.rem(z + r, NZ)
        return pltpu.make_async_remote_copy(
            tot.at[pl.ds(pl.multiple_of(there * STATE_PIECE, STATE_PIECE), STATE_PIECE)],
            p1.at[z], zs_s.at[r], zs_r.at[r], device_id=to, device_id_type=MESH,
        )

    for r in ZZ:
        zs(r).start()
    piece_at = pl.ds(pl.multiple_of(z * STATE_PIECE, STATE_PIECE), STATE_PIECE)
    p1[z] = tot[piece_at, :]

    def queries(i, carry):
        for a in range(2):
            row = pl.multiple_of(i * BLK, BLK)
            rows = pl.ds(a * HALF + row, BLK)
            q = silu(projected(0, a, row, pl.ds(0, WIDTH))).astype(BF16)
            q_ref[rows, :] = q
            for h in range(HEADS):
                grow = jnp.exp(ccol[h, rows, :])
                qs_ref[rows, h * HD : (h + 1) * HD] = (
                    q[:, h * HD : (h + 1) * HD].astype(F32) * grow
                ).astype(BF16)
        return carry

    tri = lax.broadcasted_iota(jnp.int32, (BLK, BLK), 0) >= lax.broadcasted_iota(
        jnp.int32, (BLK, BLK), 1
    )

    def attend(h, carry):
        at = pl.ds(pl.multiple_of(h * HD, HD), HD)
        for b in range(TOK // BLK):
            rows = pl.ds(b * BLK, BLK)
            q = q_ref[rows, at]
            col = ccol[h, rows, :]
            col = jnp.concatenate([col, col], axis=1)
            acc = jnp.zeros((BLK, HD), F32)
            for s in range(b + 1):
                cols = pl.ds(s * BLK, BLK)
                spread = col - cum[pl.ds(h, 1), cols]
                if s == b:
                    spread = jnp.where(tri, spread, -1e30)
                score = jnp.dot(q, kt_ref[at, cols], preferred_element_type=F32)
                weight = (jnp.exp(spread) * score).astype(BF16)
                acc = acc + jnp.dot(weight, v_ref[cols, at], preferred_element_type=F32)
            inside[rows, at] = acc
        return carry

    lax.fori_loop(0, HALF // BLK, queries, 0)
    lax.fori_loop(0, HEADS // 2, attend, 0)

    for r in ZZ:
        zs(r).wait_recv()
    head = c * 2 + z // (NZ // 2)
    state = jnp.zeros((STATE_PIECE, HD), F32)
    for k in range(NZ):
        pre[k] = state.astype(BF16)
        state = jnp.exp(dl_chip[k, pl.ds(head, 1), :]) * state + p1[k].astype(F32)

    def zg(r):
        there = lax.rem(z + r, NZ)
        return pltpu.make_async_remote_copy(
            pre.at[there], c2.at[piece_at], zg_s.at[r], zg_r.at[r],
            device_id=along(r), device_id_type=MESH,
        )

    for r in ZZ:
        zg(r).start()
    c2[piece_at, :] = pre[z]
    lax.fori_loop(HEADS // 2, HEADS, attend, 0)
    for r in XY:
        ag(r).wait_send()
    for r in ZZ:
        zs(r).wait_send()
    for r in ZZ:
        zg(r).wait_recv()

    for e in range(2):
        rows = pl.ds(e * HD, HD)
        at = pl.ds(pl.multiple_of(c * PAIR + e * HD, HD), HD)
        own = loc[at, :]
        before = c2[rows, :].astype(F32)
        even_decay = jnp.where(even, per_row(dl_own, e), per_row(dl_peer, e))
        after = even_decay * before + jnp.where(even, own, loc_recv[rows, :].astype(F32))
        loc_send[rows, :] = jnp.where(even, after, before).astype(BF16)
        here = jnp.where(even, before, after)
        carried[at, :] = here.astype(BF16)
        st_v[at, :] = per_row(dl_own, e) * here + own
    swap_carried = pltpu.make_async_remote_copy(
        loc_send, carried.at[ours], core_s.at[2], core_r.at[2],
        device_id=peer, device_id_type=MESH,
    )
    swap_carried.start()

    def write(pair, b, slot):
        rows = pl.ds(b * BLK, BLK)
        lanes = pl.ds(pl.multiple_of(pair * PAIR, PAIR), PAIR)
        return pltpu.make_async_copy(
            out_v.at[rows, lanes], out_hbm.at[rows, lanes], out_sem.at[slot]
        )

    def finish(pair, slot):
        for b in range(TOK // BLK):
            rows = pl.ds(b * BLK, BLK)
            for e in range(2):
                at = pl.ds(pl.multiple_of(pair * PAIR + e * HD, HD), HD)
                att = inside[rows, at] + jnp.dot(
                    qs_ref[rows, at], carried[at, :], preferred_element_type=F32
                )
                square = jnp.mean(att * att, axis=-1, keepdims=True)
                out_v[rows, at] = (
                    att * lax.rsqrt(square + 1e-6) * gain[pl.ds(pair * 2 + e, 1), :]
                ).astype(BF16)
            write(pair, b, slot * 4 + b).start()

    finish(c, 0)
    swap_carried.wait()
    for e in range(2):
        at = pl.ds(pl.multiple_of((1 - c) * PAIR + e * HD, HD), HD)
        decay = jnp.exp(dl_own[pl.ds((1 - c) * 2 + e, 1), :])
        st_v[at, :] = decay * carried[at, :].astype(F32) + loc[at, :]
    store_state = pltpu.make_async_copy(st_v, st_hbm, st_sem)
    store_state.start()
    finish(1 - c, 1)
    for r in ZZ:
        zg(r).wait_send()
    for b in range(TOK // BLK):
        write(c, b, b).wait()
        write(1 - c, b, 4 + b).wait()
    store_state.wait()


def local(hidden, base, down, up, decay, gain):
    anyspace = pl.BlockSpec(memory_space=pl.ANY)
    dma = pltpu.SemaphoreType.DMA
    scratch = [
        pltpu.VMEM((TOK, GROUP), BF16),
        pltpu.VMEM((3, TOK, WIDTH), BF16),
        pltpu.VMEM((3 * RANK, GROUP), BF16),
        pltpu.VMEM((3, 3 * RANK, WIDTH), BF16),
        pltpu.VMEM((HEADS, TOK), F32),
        pltpu.VMEM((HEADS, HD), F32),
        pltpu.VMEM((HALF, 2 * RANK), BF16),
        pltpu.VMEM((NTP, LORA_PIECE, 2 * RANK), BF16),
        pltpu.VMEM((HALF, 2 * RANK), BF16),
        pltpu.VMEM((8, TOK), F32),
        pltpu.VMEM((8, TOK), F32),
        pltpu.VMEM((HEADS, TOK, HD), F32),
        pltpu.VMEM((8, HD), F32),
        pltpu.VMEM((8, HD), F32),
        pltpu.VMEM((NZ, 8, HD), F32),
        pltpu.VMEM((TOK, WIDTH), BF16),
        pltpu.VMEM((TOK, WIDTH), BF16),
        pltpu.VMEM((WIDTH, TOK), BF16),
        pltpu.VMEM((TOK, WIDTH), BF16),
        pltpu.VMEM((TOK, WIDTH), F32),
        pltpu.VMEM((TOK, WIDTH), BF16),
        pltpu.VMEM((WIDTH, HD), F32),
        pltpu.VMEM((PAIR, HD), BF16),
        pltpu.VMEM((PAIR, HD), BF16),
        pltpu.VMEM((PAIR, HD), BF16),
        pltpu.VMEM((NZ, STATE_PIECE, HD), BF16),
        pltpu.VMEM((NZ, STATE_PIECE, HD), BF16),
        pltpu.VMEM((PAIR, HD), BF16),
        pltpu.VMEM((WIDTH, HD), BF16),
        pltpu.VMEM((WIDTH, HD), F32),
        dma((6,)), dma((8,)), dma,
        dma((NTP,)), dma((NTP,)), dma((NTP,)), dma((NTP,)),
        dma((NZ,)), dma((NZ,)), dma((NZ,)), dma((NZ,)), dma((NZ,)), dma((NZ,)),
        dma((3,)), dma((3,)),
    ]
    mixed, states = pl.pallas_call(
        kernel,
        out_shape=(
            jax.ShapeDtypeStruct((TOK, WIDTH), BF16),
            jax.ShapeDtypeStruct((WIDTH, HD), F32),
        ),
        in_specs=[anyspace] * 6,
        out_specs=(anyspace, anyspace),
        scratch_shapes=scratch,
        compiler_params=pltpu.CompilerParams(
            collective_id=0, has_side_effects=True, vmem_limit_bytes=48 * 1024 * 1024
        ),
        cost_estimate=pl.CostEstimate(
            flops=3_000_000_000, bytes_accessed=6_000_000, transcendentals=6_000_000
        ),
    )(hidden, base, down.T, up, decay.T, gain.reshape(HEADS, HD))
    return mixed, states.reshape(1, HEADS, HD, HD)


def solution(mesh):
    in_specs = (
        P("ctx", "tp"),
        P(None, "ctx", "tp"),
        P("tp", None),
        P(None, None, "tp"),
        P("ctx", "tp"),
        P("tp"),
    )
    out_specs = (P("ctx", "tp"), P("ctx", "tp", None, None))
    return jax.shard_map(local, mesh=mesh, in_specs=in_specs, out_specs=out_specs, check_vma=False)
```

time: 265 us -> 56.9 us (0.21)
  waiting for transfers between devices: 118 us -> 0 us
  Pallas kernels: 0 us -> 48.1 us
  other arithmetic: 40.2 us -> 0 us
  blocking collectives: 32.9 us -> 0 us
  matrix products: 23.7 us -> 0 us
  local copies, waits for them, and re-layouts: 23.1 us -> 7.81 us
  between operations: 14.2 us -> 0.65 us
  loops' own time: 12.1 us -> 0 us
    psum x1 -> x0, waiting for transfers between devices: 111 us -> none  [local(): lax.psum(partial_output_rows.astype(jnp.bfloat16), 'tp')]
    pallas_call x0 -> x1, Pallas kernels: none -> 48.1 us  [local(): pl.pallas_call(kernel, out_shape=(jax.ShapeDtypeStruct((TOK, WIDTH), BF16...]
    all_gather x1 -> x0, blocking collectives: 32.9 us -> none  [prefix(): lax.all_gather(part.astype(kind), axis)]
    select_n x32 -> x0, other arithmetic: 32.4 us -> none  [hop(): return jax.tree.map(lambda a, b: jnp.where(reached, a, b), new, before)]
    dot_general x8 -> x0, matrix products: 23.7 us -> none  [the longest x4 12.5 us: one_head(): return jnp.dot(weights, value_head, preferred_element_type=jnp.float32)]
    another operation x2 -> x0, loops' own time: 12.1 us -> none  [the longest x1 11.1 us: local(): lax.map(one_head, jnp.arange(head_number_total, dtype=jnp.int32))]
    all_gather x1 -> x0, waiting for transfers between devices: 6.43 us -> none  [prefix(): lax.all_gather(part.astype(kind), axis)]
    convert_element_type x35 -> x0, other arithmetic: 5.52 us -> none  [the longest x1 4.74 us: local(): key_rows = jax.nn.silu(projected_rows[1]).astype(jnp.bfloat16)]
  transfers between devices with their start and end apart: 2 -> 0, of which waited for: 2 -> 0; matrix products, arithmetic and copies ran while one was open for 12% -> 0% of each run, Pallas kernels for 0% -> 0%
where the time goes in v1:
time: 56.9 us; the launch traced here: 56.5 us
  Pallas kernels  48.1 us (85%)
  local copies, waits for them, and re-layouts  7.81 us (14%)
  between operations  0.65 us (1%)
    pallas_call x1, Pallas kernels, local(): pl.pallas_call(kernel, out_shape=(jax.ShapeDtypeStruct((TOK, WIDTH), BF16...  48.1 us
    unnamed x14, local copies, waits for them, and re-layouts  7.81 us

profile of v1, /device:TPU:1, one launch (start us, length us, event | category | flops | bytes accessed | tf_op | source)
XLA Modules:
  0.0 56.5 jit_solution(10291424055660852919)
XLA Ops:
  0.6 0.0 copy-start
  0.6 1.9 %copy-done = bf16[3,1024,512]{2,1,0:T(8,128)(2,1)S(1)} copy-done((bf16[3,1024,512]{2,1,0:T(8,128)(2,1)S(1)}, bf16[3,1024,512]{2,1,0:T(8,128)(2,1)}, u32[]{:S(2)}) %copy-start) | copy-done | bytes 3145752
  2.5 0.0 copy-start.1
  2.5 1.1 %copy-done.1 = bf16[1024,384]{1,0:T(8,128)(2,1)S(1)} copy-done((bf16[1024,384]{1,0:T(8,128)(2,1)S(1)}, bf16[1024,384]{1,0:T(8,128)(2,1)}, u32[]{:S(2)}) %copy-start.1) | copy-done | bytes 786456
  3.7 0.0 copy-start.2
  3.7 0.9 %copy-done.2 = bf16[3,64,512]{2,1,0:T(8,128)(2,1)S(1)} copy-done((bf16[3,64,512]{2,1,0:T(8,128)(2,1)S(1)}, bf16[3,64,512]{2,1,0:T(8,128)(2,1)}, u32[]{:S(2)}) %copy-start.2) | copy-done | bytes 196632
  4.6 0.0 copy-start.3
  4.6 0.8 %copy-done.3 = bf16[384,64]{0,1:T(8,128)(2,1)S(1)} copy-done((bf16[384,64]{0,1:T(8,128)(2,1)S(1)}, bf16[384,64]{0,1:T(8,128)(2,1)}, u32[]{:S(2)}) %copy-start.3) | copy-done | bytes 49176
  5.4 0.0 copy-start.4
  5.4 0.7 %copy-done.4 = f32[1024,4]{0,1:T(4,128)S(1)} copy-done((f32[1024,4]{0,1:T(4,128)S(1)}, f32[1024,4]{0,1:T(4,128)}, u32[]{:S(2)}) %copy-start.4) | copy-done | bytes 16408
  6.1 0.0 copy-start.5
  6.1 0.7 %copy-done.5 = f32[512]{0:T(512)S(1)} copy-done((f32[512]{0:T(512)S(1)}, f32[512]{0:T(512)}, u32[]{:S(2)}) %copy-start.5) | copy-done | bytes 2072
  6.8 48.1 %shard_map.77 = (bf16[1024,512]{1,0:T(8,128)(2,1)S(1)}, f32[512,128]{1,0:T(8,128)S(1)}) custom-call(bf16[1024,384]{1,0:T(8,128)(2,1)S(1)} %copy-done.1, bf16[3,1024,512]{2,1,0:T(8,128)(2,1)S(1)} %copy-done, bf16[64,384]{1,0:T(8,128)(2,1)S(1)} %bitcast.5, bf16[3,64,512]{2,1,0:T(8,128)(2,1)S(1)} %copy-done.2, f32[4,1024]{1,0:T(4,128)S(1)} %bitcast.6, ...), custom_call_target="tpu_custom_call" | custom-call | flops 3000000000 | bytes 6000000 | tf_op jit(solution)/shard_map/pallas_call | solution.py:389
  54.8 1.0 %copy.10 = bf16[1024,512]{1,0:T(8,128)(2,1)} copy(bf16[1024,512]{1,0:T(8,128)(2,1)S(1)} %get-tuple-element.8) | data formatting | bytes 2097152
  55.8 0.7 %copy.11 = f32[1,4,128,128]{3,2,1,0:T(8,128)} copy(f32[1,4,128,128]{3,2,1,0:T(8,128)S(1)} %bitcast.4) | data formatting | bytes 524288
Async XLA Ops:
  0.6 1.9 %copy-start = (bf16[3,1024,512]{2,1,0:T(8,128)(2,1)S(1)}, bf16[3,1024,512]{2,1,0:T(8,128)(2,1)}, u32[]{:S(2)}) copy-start(bf16[3,1024,512]{2,1,0:T(8,128)(2,1)} %base_hbm.1) | copy-start | bytes 9437188
  2.5 1.1 %copy-start.1 = (bf16[1024,384]{1,0:T(8,128)(2,1)S(1)}, bf16[1024,384]{1,0:T(8,128)(2,1)}, u32[]{:S(2)}) copy-start(bf16[1024,384]{1,0:T(8,128)(2,1)} %hid_hbm.1) | copy-start | bytes 2359300
  3.7 0.9 %copy-start.2 = (bf16[3,64,512]{2,1,0:T(8,128)(2,1)S(1)}, bf16[3,64,512]{2,1,0:T(8,128)(2,1)}, u32[]{:S(2)}) copy-start(bf16[3,64,512]{2,1,0:T(8,128)(2,1)} %up_hbm.1) | copy-start | bytes 589828
  4.6 0.8 %copy-start.3 = (bf16[384,64]{0,1:T(8,128)(2,1)S(1)}, bf16[384,64]{0,1:T(8,128)(2,1)}, u32[]{:S(2)}) copy-start(bf16[384,64]{0,1:T(8,128)(2,1)} %param.8) | copy-start | bytes 147460
  5.4 0.7 %copy-start.4 = (f32[1024,4]{0,1:T(4,128)S(1)}, f32[1024,4]{0,1:T(4,128)}, u32[]{:S(2)}) copy-start(f32[1024,4]{0,1:T(4,128)} %param.10) | copy-start | bytes 49156
  6.1 0.7 %copy-start.5 = (f32[512]{0:T(512)S(1)}, f32[512]{0:T(512)}, u32[]{:S(2)}) copy-start(f32[512]{0:T(512)} %param.11) | copy-start | bytes 6148

commit v2 on v1

--- a/solution.py
+++ b/solution.py
@@ -17,7 +17,9 @@
 NX, NY, NZ = 4, 4, 16
 NTP = NX * NY
 LORA_PIECE = HALF // NTP
-STATE_PIECE = PAIR // NZ
+CHUNK = HALF // NX
+HZ = NZ // 2
+STATE_PIECE = PAIR // HZ
 MESH = pl.DeviceIdType.MESH
 F32, BF16 = jnp.float32, jnp.bfloat16
 
@@ -27,7 +29,14 @@
 
 
 XY = sorted(range(1, NTP), key=lambda r: -(ring(r // NY, NX) + ring(r % NY, NY)))
-ZZ = sorted(range(1, NZ), key=lambda r: -ring(r, NZ))
+ZH = [4, 3, 5, 2, 6, 1, 7]
+
+
+def order(z):
+    return jnp.where(z < HZ, z, jnp.where(z >= 12, 23 - z, z + 4))
+
+
+ORDER = [z if z < HZ else (23 - z if z >= 12 else z + 4) for z in range(NZ)]
 
 
 def silu(v):
@@ -44,7 +53,7 @@
     q_ref, qs_ref, kt_ref, v_ref, inside, out_v,
     loc, loc_send, loc_recv, tot, p1, pre, c2, carried, st_v,
     in_sem, out_sem, st_sem,
-    rs_s, rs_r, ag_s, ag_r, zs_s, zs_r, zg_s, zg_r, dz_s, dz_r, core_s, core_r,
+    rs_s, rs_r, ag_s, ag_r, zs_s, zs_r, zg_s, zg_r, dz_s, dz_r, core_s, core_r, near_sem, far_sem,
 ):
     ctx, tp = lax.axis_index("ctx"), lax.axis_index("tp")
     z, c = ctx // 2, ctx % 2
@@ -54,15 +63,25 @@
     def plane(r):
         return {"tp": lax.rem(x + r // NY, NX) * NY + lax.rem(y + r % NY, NY)}
 
+    zh = z % HZ
+    base_z = z - zh
+    lower = z < HZ
+
+    def chip(other):
+        return {"ctx": other * 2 + c}
+
     def along(r):
-        return {"ctx": lax.rem(z + r, NZ) * 2 + c}
-
+        return base_z + lax.rem(zh + r, HZ)
+
+    place = order(z)
     barrier = pltpu.get_barrier_semaphore()
-    for r in ZZ:
-        pl.semaphore_signal(barrier, inc=1, device_id=along(r), device_id_type=MESH)
     for r in XY:
         pl.semaphore_signal(barrier, inc=1, device_id=plane(r), device_id_type=MESH)
     pl.semaphore_signal(barrier, inc=1, device_id=peer, device_id_type=MESH)
+    for k in range(NZ):
+        @pl.when(place < ORDER[k])
+        def _(k=k):
+            pl.semaphore_signal(barrier, inc=1, device_id=chip(k), device_id_type=MESH)
 
     loads = [
         pltpu.make_async_copy(dwn_hbm, dpad.at[pl.ds(RANK, RANK)], in_sem.at[0]),
@@ -96,7 +115,7 @@
         )
         part[rows, :] = mine.astype(BF16)
 
-    pl.semaphore_wait(barrier, NTP - 1 + NZ - 1 + 1)
+    pl.semaphore_wait(barrier, NTP - 1 + 1 + place)
 
     def rs(r):
         to = plane(r)
@@ -107,6 +126,17 @@
 
     for r in XY:
         rs(r).start()
+
+    for k in range(NZ):
+        same = lower if k < HZ else jnp.logical_not(lower)
+
+        @pl.when(jnp.logical_and(place > ORDER[k], same))
+        def _(k=k):
+            pl.semaphore_signal(near_sem, inc=1, device_id=chip(k), device_id_type=MESH)
+
+        @pl.when(jnp.logical_and(place > ORDER[k], jnp.logical_not(same)))
+        def _(k=k):
+            pl.semaphore_signal(far_sem, inc=1, device_id=chip(k), device_id_type=MESH)
 
     loads[2].wait()
     run = jnp.concatenate([dec[...], jnp.zeros((8 - HEADS, TOK), F32)], axis=0)
@@ -133,14 +163,17 @@
     swap_decay.wait()
     dl_chip[z] = dl_own[...] + dl_peer[...]
 
-    def dz(r):
-        return pltpu.make_async_remote_copy(
-            dl_chip.at[z], dl_chip.at[z], dz_s.at[r], dz_r.at[r],
-            device_id=along(r), device_id_type=MESH,
-        )
-
-    for r in ZZ:
-        dz(r).start()
+    def dz(other, slot):
+        return pltpu.make_async_remote_copy(
+            dl_chip.at[z], dl_chip.at[z], dz_s.at[slot], dz_r.at[z],
+            device_id=chip(other), device_id_type=MESH,
+        )
+
+    def dz_from(k):
+        return pltpu.make_async_remote_copy(
+            dl_chip.at[k], dl_chip.at[k], dz_s.at[0], dz_r.at[k],
+            device_id=peer, device_id_type=MESH,
+        )
 
     mine_at = pl.ds(pl.multiple_of(tp * LORA_PIECE, LORA_PIECE), LORA_PIECE)
     for r in XY:
@@ -160,46 +193,68 @@
         ag(r).start()
     for r in XY:
         rs(r).wait_send()
-    for r in ZZ:
-        dz(r).wait()
+    later = jnp.where(lower, HZ, NZ) - 1 - place
+
+    @pl.when(later > 0)
+    def _():
+        pl.semaphore_wait(near_sem, later)
+
+    for r in ZH:
+        dz(along(r), r).start()
     loads[3].wait()
     loads[4].wait()
     loads[5].wait()
-    for r in XY:
-        ag(r).wait_recv()
-
-    def projected(i, a, row, lanes):
-        return base[i, pl.ds(a * HALF + row, BLK), lanes].astype(F32) + jnp.dot(
-            lora[pl.ds(row, BLK), :],
+
+    def projected(i, a, row, size, lanes):
+        return base[i, pl.ds(a * HALF + row, size), lanes].astype(F32) + jnp.dot(
+            lora[pl.ds(row, size), :],
             upad[i, pl.ds(RANK - RANK * a, 2 * RANK), lanes],
             preferred_element_type=F32,
         )
 
-    def keys_values(pair):
-        lanes = pl.ds(pl.multiple_of(pair * PAIR, PAIR), PAIR)
+    for n, shift in enumerate((0, 1, 3, 2)):
+        for ry in range(NY):
+            if shift or ry:
+                ag(shift * NY + ry).wait_recv()
+        row = pl.multiple_of(lax.rem(x + NX - shift, NX) * CHUNK, CHUNK)
+        scaled = []
         for a in range(2):
-            for row in range(0, HALF, BLK):
-                rows = pl.ds(a * HALF + row, BLK)
-                k = silu(projected(1, a, row, lanes)).astype(BF16)
-                kt_ref[lanes, rows] = k.T
-                v_ref[rows, lanes] = projected(2, a, row, lanes).astype(BF16)
-        for e in range(2):
-            h = pair * 2 + e
-            at = pl.ds(pl.multiple_of(h * HD, HD), HD)
-            scaled = (kt_ref[at, :].astype(F32) * wgt[pl.ds(h, 1), :]).astype(BF16)
-            loc[at, :] = jnp.dot(scaled, v_ref[:, at], preferred_element_type=F32)
+            at = pl.ds(pl.multiple_of(a * HALF + row, CHUNK), CHUNK)
+            k = silu(projected(1, a, row, CHUNK, slice(None))).astype(BF16).T
+            kt_ref[:, at] = k
+            v_ref[at, :] = projected(2, a, row, CHUNK, slice(None)).astype(BF16)
+            scaled.append(
+                [
+                    (k[h * HD : (h + 1) * HD].astype(F32) * wgt[h : h + 1, at]).astype(BF16)
+                    for h in range(HEADS)
+                ]
+            )
+        for h in range(HEADS):
+            lanes = slice(h * HD, (h + 1) * HD)
+            part_sum = sum(
+                jnp.dot(
+                    scaled[a][h],
+                    v_ref[pl.ds(pl.multiple_of(a * HALF + row, CHUNK), CHUNK), lanes],
+                    preferred_element_type=F32,
+                )
+                for a in range(2)
+            )
+            if n == 0:
+                loc[lanes, :] = part_sum
+            else:
+                loc[lanes, :] += part_sum
 
     ours = pl.ds(pl.multiple_of(c * PAIR, PAIR), PAIR)
     theirs = pl.ds(pl.multiple_of((1 - c) * PAIR, PAIR), PAIR)
     even = c == 0
 
-    keys_values(1 - c)
     loc_send[...] = loc[theirs, :].astype(BF16)
     swap_local = pltpu.make_async_remote_copy(
         loc_send, loc_recv, core_s.at[1], core_r.at[1], device_id=peer, device_id_type=MESH
     )
     swap_local.start()
-    keys_values(c)
+    for r in ZH:
+        dz(along(r), r).wait_send()
     swap_local.wait()
 
     def per_row(ref, e):
@@ -214,24 +269,39 @@
             jnp.where(even, own, other) * odd_decay + jnp.where(even, other, own)
         ).astype(BF16)
 
-    def zs(r):
-        to = along(r)
-        there = lax.rem(z + r, NZ)
-        return pltpu.make_async_remote_copy(
-            tot.at[pl.ds(pl.multiple_of(there * STATE_PIECE, STATE_PIECE), STATE_PIECE)],
-            p1.at[z], zs_s.at[r], zs_r.at[r], device_id=to, device_id_type=MESH,
-        )
-
-    for r in ZZ:
-        zs(r).start()
-    piece_at = pl.ds(pl.multiple_of(z * STATE_PIECE, STATE_PIECE), STATE_PIECE)
+    def zs(other, slot):
+        rows = pl.ds(pl.multiple_of((other % HZ) * STATE_PIECE, STATE_PIECE), STATE_PIECE)
+        return pltpu.make_async_remote_copy(
+            tot.at[rows], p1.at[z], zs_s.at[slot], zs_r.at[z],
+            device_id=chip(other), device_id_type=MESH,
+        )
+
+    def zs_from(k):
+        return pltpu.make_async_remote_copy(
+            tot.at[pl.ds(0, STATE_PIECE)], p1.at[k], zs_s.at[0], zs_r.at[k],
+            device_id=peer, device_id_type=MESH,
+        )
+
+    @pl.when(zh < HZ - 1)
+    def _():
+        for r in ZH:
+            zs(along(r), r).start()
+
+    @pl.when(lower)
+    def _():
+        pl.semaphore_wait(far_sem, HZ)
+        for r in range(HZ):
+            dz(HZ + lax.rem(z + r, HZ), HZ + r).start()
+            zs(HZ + lax.rem(z + r, HZ), HZ + r).start()
+
+    piece_at = pl.ds(pl.multiple_of(zh * STATE_PIECE, STATE_PIECE), STATE_PIECE)
     p1[z] = tot[piece_at, :]
 
     def queries(i, carry):
         for a in range(2):
             row = pl.multiple_of(i * BLK, BLK)
             rows = pl.ds(a * HALF + row, BLK)
-            q = silu(projected(0, a, row, pl.ds(0, WIDTH))).astype(BF16)
+            q = silu(projected(0, a, row, BLK, slice(None))).astype(BF16)
             q_ref[rows, :] = q
             for h in range(HEADS):
                 grow = jnp.exp(ccol[h, rows, :])
@@ -266,31 +336,85 @@
     lax.fori_loop(0, HALF // BLK, queries, 0)
     lax.fori_loop(0, HEADS // 2, attend, 0)
 
-    for r in ZZ:
-        zs(r).wait_recv()
-    head = c * 2 + z // (NZ // 2)
-    state = jnp.zeros((STATE_PIECE, HD), F32)
-    for k in range(NZ):
-        pre[k] = state.astype(BF16)
-        state = jnp.exp(dl_chip[k, pl.ds(head, 1), :]) * state + p1[k].astype(F32)
+    head = c * 2 + zh // (HZ // 2)
+
+    def arrive(k):
+        @pl.when(z != k)
+        def _():
+            dz_from(k).wait_recv()
+            zs_from(k).wait_recv()
+
+    def advance(state, k):
+        return jnp.exp(dl_chip[k, pl.ds(head, 1), :]) * state + p1[k].astype(F32)
 
     def zg(r):
-        there = lax.rem(z + r, NZ)
-        return pltpu.make_async_remote_copy(
-            pre.at[there], c2.at[piece_at], zg_s.at[r], zg_r.at[r],
-            device_id=along(r), device_id_type=MESH,
-        )
-
-    for r in ZZ:
-        zg(r).start()
-    c2[piece_at, :] = pre[z]
+        return pltpu.make_async_remote_copy(
+            pre.at[lax.rem(zh + r, HZ)], c2.at[piece_at], zg_s.at[r], zg_r.at[r],
+            device_id=chip(along(r)), device_id_type=MESH,
+        )
+
+    def gather(r, what):
+        @pl.when(along(r) != 0)
+        def _():
+            what(zg(r))
+
+    @pl.when(lower)
+    def _():
+        for k in range(HZ - 1):
+            arrive(k)
+
+        @pl.when(z < HZ - 1)
+        def _():
+            dz_from(HZ - 1).wait_recv()
+
+        state = jnp.zeros((STATE_PIECE, HD), F32)
+        for k in range(HZ - 1):
+            pre[k] = state.astype(BF16)
+            state = advance(state, k)
+        pre[HZ - 1] = state.astype(BF16)
+
+    @pl.when(jnp.logical_not(lower))
+    def _():
+        for k in range(NZ - 1):
+            arrive(k)
+
+        @pl.when(z < NZ - 1)
+        def _():
+            dz_from(NZ - 1).wait_recv()
+
+        state = jnp.zeros((STATE_PIECE, HD), F32)
+        for k in range(NZ - 1):
+            if k >= HZ:
+                pre[k - HZ] = state.astype(BF16)
+            state = advance(state, k)
+        pre[HZ - 1] = state.astype(BF16)
+
+    for r in ZH:
+        gather(r, lambda copy: copy.start())
+    c2[piece_at, :] = pre[zh]
     lax.fori_loop(HEADS // 2, HEADS, attend, 0)
     for r in XY:
         ag(r).wait_send()
-    for r in ZZ:
-        zs(r).wait_send()
-    for r in ZZ:
-        zg(r).wait_recv()
+
+    @pl.when(zh < HZ - 1)
+    def _():
+        for r in ZH:
+            zs(along(r), r).wait_send()
+
+    @pl.when(lower)
+    def _():
+        for r in range(HZ):
+            dz(HZ + lax.rem(z + r, HZ), HZ + r).wait_send()
+            zs(HZ + lax.rem(z + r, HZ), HZ + r).wait_send()
+
+    @pl.when(z != 0)
+    def _():
+        for r in ZH:
+            zg(r).wait_recv()
+
+    @pl.when(z == 0)
+    def _():
+        c2[...] = jnp.zeros_like(c2)
 
     for e in range(2):
         rows = pl.ds(e * HD, HD)
@@ -339,8 +463,8 @@
     store_state = pltpu.make_async_copy(st_v, st_hbm, st_sem)
     store_state.start()
     finish(1 - c, 1)
-    for r in ZZ:
-        zg(r).wait_send()
+    for r in ZH:
+        gather(r, lambda copy: copy.wait_send())
     for b in range(TOK // BLK):
         write(c, b, b).wait()
         write(1 - c, b, 4 + b).wait()
@@ -377,14 +501,14 @@
         pltpu.VMEM((PAIR, HD), BF16),
         pltpu.VMEM((PAIR, HD), BF16),
         pltpu.VMEM((NZ, STATE_PIECE, HD), BF16),
-        pltpu.VMEM((NZ, STATE_PIECE, HD), BF16),
+        pltpu.VMEM((HZ, STATE_PIECE, HD), BF16),
         pltpu.VMEM((PAIR, HD), BF16),
         pltpu.VMEM((WIDTH, HD), BF16),
         pltpu.VMEM((WIDTH, HD), F32),
         dma((6,)), dma((8,)), dma,
         dma((NTP,)), dma((NTP,)), dma((NTP,)), dma((NTP,)),
         dma((NZ,)), dma((NZ,)), dma((NZ,)), dma((NZ,)), dma((NZ,)), dma((NZ,)),
-        dma((3,)), dma((3,)),
+        dma((3,)), dma((3,)), pltpu.SemaphoreType.REGULAR, pltpu.SemaphoreType.REGULAR,
     ]
     mixed, states = pl.pallas_call(
         kernel,
@@ -401,7 +525,7 @@
         cost_estimate=pl.CostEstimate(
             flops=3_000_000_000, bytes_accessed=6_000_000, transcendentals=6_000_000
         ),
-    )(hidden, base, down.T, up, decay.T, gain.reshape(HEADS, HD))
+    )(*[pltpu.with_memory_space_constraint(a, pltpu.HBM) for a in (hidden, base, down.T, up, decay.T, gain.reshape(HEADS, HD))])
     return mixed, states.reshape(1, HEADS, HD, HD)
 
 

time: 56.9 us -> 43.8 us (0.77)
  the two profiles are of different devices: /device:TPU:1 before, /device:TPU:257 now
where the time goes in v2:
time: 43.8 us; the launch traced here: 43.7 us
  Pallas kernels  41.4 us (95%)
  local copies, waits for them, and re-layouts  1.67 us (4%)
  between operations  0.64 us (1%)
    pallas_call x1, Pallas kernels, local(): pl.pallas_call(kernel, out_shape=(jax.ShapeDtypeStruct((TOK, WIDTH), BF16...  41.4 us
    unnamed x2, local copies, waits for them, and re-layouts  1.67 us

profile of v2, /device:TPU:257, one launch (start us, length us, event | category | flops | bytes accessed | tf_op | source)
XLA Modules:
  0.0 43.7 jit_solution(3490256570719487091)
XLA Ops:
  0.6 41.4 %shard_map.77 = (bf16[1024,512]{1,0:T(8,128)(2,1)S(1)}, f32[512,128]{1,0:T(8,128)S(1)}) custom-call(bf16[1024,384]{1,0:T(8,128)(2,1)} %hid_hbm.1, bf16[3,1024,512]{2,1,0:T(8,128)(2,1)} %base_hbm.1, bf16[64,384]{1,0:T(8,128)(2,1)} %bitcast.5, bf16[3,64,512]{2,1,0:T(8,128)(2,1)} %up_hbm.1, f32[4,1024]{1,0:T(4,128)} %bitcast.6, f32[4,128]{1,0:T(4,128)} %bitcast.7), custom_call_target="tpu_custom_call" | custom-call | flops 3000000000 | bytes 6000000 | tf_op jit(solution)/shard_map/pallas_call | solution.py:513
  42.0 1.0 %copy.10 = bf16[1024,512]{1,0:T(8,128)(2,1)} copy(bf16[1024,512]{1,0:T(8,128)(2,1)S(1)} %get-tuple-element.8) | data formatting | bytes 2097152
  43.0 0.7 %copy.11 = f32[1,4,128,128]{3,2,1,0:T(8,128)} copy(f32[1,4,128,128]{3,2,1,0:T(8,128)S(1)} %bitcast.4) | data formatting | bytes 524288

commit v3 on v2

--- a/solution.py
+++ b/solution.py
@@ -19,7 +19,11 @@
 LORA_PIECE = HALF // NTP
 CHUNK = HALF // NX
 HZ = NZ // 2
-STATE_PIECE = PAIR // HZ
+OWNERS = 4
+FIRST = 2
+EARLY = 5
+STATE_PIECE = PAIR // OWNERS
+LANES = HD // HEADS
 MESH = pl.DeviceIdType.MESH
 F32, BF16 = jnp.float32, jnp.bfloat16
 
@@ -46,13 +50,13 @@
 
 def kernel(
     hid_hbm, base_hbm, dwn_hbm, up_hbm, dec_hbm, gain_hbm,
-    out_hbm, st_hbm,
+    out_v, st_v,
     hid, base, dpad, upad, dec, gain,
     part, rsum, lora,
-    cum, wgt, ccol, dl_own, dl_peer, dl_chip,
-    q_ref, qs_ref, kt_ref, v_ref, inside, out_v,
-    loc, loc_send, loc_recv, tot, p1, pre, c2, carried, st_v,
-    in_sem, out_sem, st_sem,
+    cum, wgt, ccol, dl_own, dl_peer, dl_chip, chip_decay,
+    q_ref, qs_ref, kt_ref, v_ref, inside,
+    loc, loc_send, loc_recv, tot, p1, pre, c2, carried,
+    in_sem,
     rs_s, rs_r, ag_s, ag_r, zs_s, zs_r, zg_s, zg_r, dz_s, dz_r, core_s, core_r, near_sem, far_sem,
 ):
     ctx, tp = lax.axis_index("ctx"), lax.axis_index("tp")
@@ -134,7 +138,7 @@
         def _(k=k):
             pl.semaphore_signal(near_sem, inc=1, device_id=chip(k), device_id_type=MESH)
 
-        @pl.when(jnp.logical_and(place > ORDER[k], jnp.logical_not(same)))
+        @pl.when(jnp.logical_and(place > ORDER[k], jnp.logical_and(jnp.logical_not(same), k >= FIRST)))
         def _(k=k):
             pl.semaphore_signal(far_sem, inc=1, device_id=chip(k), device_id_type=MESH)
 
@@ -161,12 +165,19 @@
     lax.fori_loop(0, HEADS, ccol_of, 0)
 
     swap_decay.wait()
-    dl_chip[z] = dl_own[...] + dl_peer[...]
-
-    def dz(other, slot):
-        return pltpu.make_async_remote_copy(
-            dl_chip.at[z], dl_chip.at[z], dz_s.at[slot], dz_r.at[z],
-            device_id=chip(other), device_id_type=MESH,
+    head_of_lane = lax.broadcasted_iota(jnp.int32, (8, HD), 1) // LANES
+    dl_chip[z] = jnp.sum(
+        jnp.where(
+            head_of_lane == lax.broadcasted_iota(jnp.int32, (8, HD), 0),
+            dl_own[...] + dl_peer[...], 0.0,
+        ),
+        axis=0, keepdims=True,
+    )
+
+    def dz(owner):
+        return pltpu.make_async_remote_copy(
+            dl_chip.at[z], dl_chip.at[z], dz_s.at[owner], dz_r.at[z],
+            device_id=chip(owner), device_id_type=MESH,
         )
 
     def dz_from(k):
@@ -174,6 +185,14 @@
             dl_chip.at[k], dl_chip.at[k], dz_s.at[0], dz_r.at[k],
             device_id=peer, device_id_type=MESH,
         )
+
+    def to_owners(half, what):
+        for k in range(OWNERS):
+            owner = half + FIRST + jnp.where(lower, k, OWNERS - 1 - k)
+
+            @pl.when(owner != z)
+            def _(owner=owner, k=k):
+                what(owner, k)
 
     mine_at = pl.ds(pl.multiple_of(tp * LORA_PIECE, LORA_PIECE), LORA_PIECE)
     for r in XY:
@@ -199,8 +218,12 @@
     def _():
         pl.semaphore_wait(near_sem, later)
 
-    for r in ZH:
-        dz(along(r), r).start()
+    adds = zh < HZ - 1
+
+    @pl.when(adds)
+    def _():
+        to_owners(base_z, lambda owner, k: dz(owner).start())
+
     loads[3].wait()
     loads[4].wait()
     loads[5].wait()
@@ -253,8 +276,10 @@
         loc_send, loc_recv, core_s.at[1], core_r.at[1], device_id=peer, device_id_type=MESH
     )
     swap_local.start()
-    for r in ZH:
-        dz(along(r), r).wait_send()
+    @pl.when(adds)
+    def _():
+        to_owners(base_z, lambda owner, k: dz(owner).wait_send())
+
     swap_local.wait()
 
     def per_row(ref, e):
@@ -269,11 +294,10 @@
             jnp.where(even, own, other) * odd_decay + jnp.where(even, other, own)
         ).astype(BF16)
 
-    def zs(other, slot):
-        rows = pl.ds(pl.multiple_of((other % HZ) * STATE_PIECE, STATE_PIECE), STATE_PIECE)
-        return pltpu.make_async_remote_copy(
-            tot.at[rows], p1.at[z], zs_s.at[slot], zs_r.at[z],
-            device_id=chip(other), device_id_type=MESH,
+    def zs(owner, k):
+        return pltpu.make_async_remote_copy(
+            tot.at[pl.ds(k * STATE_PIECE, STATE_PIECE)], p1.at[z], zs_s.at[owner], zs_r.at[z],
+            device_id=chip(owner), device_id_type=MESH,
         )
 
     def zs_from(k):
@@ -282,20 +306,30 @@
             device_id=peer, device_id_type=MESH,
         )
 
-    @pl.when(zh < HZ - 1)
-    def _():
-        for r in ZH:
-            zs(along(r), r).start()
-
-    @pl.when(lower)
+    @pl.when(adds)
+    def _():
+        to_owners(base_z, lambda owner, k: zs(owner, k).start())
+
+    far = jnp.logical_and(lower, z >= EARLY)
+
+    def to_far(what):
+        for k in range(OWNERS):
+            what(HZ + FIRST + OWNERS - 1 - k, k)
+
+    @pl.when(far)
     def _():
         pl.semaphore_wait(far_sem, HZ)
-        for r in range(HZ):
-            dz(HZ + lax.rem(z + r, HZ), HZ + r).start()
-            zs(HZ + lax.rem(z + r, HZ), HZ + r).start()
-
-    piece_at = pl.ds(pl.multiple_of(zh * STATE_PIECE, STATE_PIECE), STATE_PIECE)
-    p1[z] = tot[piece_at, :]
+
+        def start(owner, k):
+            dz(owner).start()
+            zs(owner, k).start()
+
+        to_far(start)
+
+    owns = jnp.logical_and(zh >= FIRST, zh < FIRST + OWNERS)
+    mine_k = jnp.where(lower, zh - FIRST, FIRST + OWNERS - 1 - zh)
+    mine_k = jnp.clip(mine_k, 0, OWNERS - 1)
+    piece_at = pl.ds(pl.multiple_of(mine_k * STATE_PIECE, STATE_PIECE), STATE_PIECE)
 
     def queries(i, carry):
         for a in range(2):
@@ -333,84 +367,118 @@
             inside[rows, at] = acc
         return carry
 
-    lax.fori_loop(0, HALF // BLK, queries, 0)
-    lax.fori_loop(0, HEADS // 2, attend, 0)
-
-    head = c * 2 + zh // (HZ // 2)
+    scan_first = jnp.logical_or(z == 4, z == 5)
+    blocks_before = jnp.where(scan_first, 0, HALF // BLK)
+    heads_before = jnp.where(scan_first, 0, HEADS // 2)
+    lax.fori_loop(0, blocks_before, queries, 0)
+    lax.fori_loop(0, heads_before, attend, 0)
+
+    head_lane = (c * 2 + mine_k // 2) * LANES
+    lane_of = lax.broadcasted_iota(jnp.int32, (1, 1, HD), 2)
 
     def arrive(k):
         @pl.when(z != k)
         def _():
-            dz_from(k).wait_recv()
             zs_from(k).wait_recv()
 
+    def decays(first, last):
+        for k in range(first, last):
+            @pl.when(z != k)
+            def _(k=k):
+                dz_from(k).wait_recv()
+
+        log = jnp.sum(
+            jnp.where(lane_of == head_lane, dl_chip[first:last], 0.0), axis=2, keepdims=True
+        )
+        chip_decay[first:last] = jnp.broadcast_to(jnp.exp(log), (last - first, 1, HD))
+
     def advance(state, k):
-        return jnp.exp(dl_chip[k, pl.ds(head, 1), :]) * state + p1[k].astype(F32)
-
-    def zg(r):
-        return pltpu.make_async_remote_copy(
-            pre.at[lax.rem(zh + r, HZ)], c2.at[piece_at], zg_s.at[r], zg_r.at[r],
-            device_id=chip(along(r)), device_id_type=MESH,
-        )
-
-    def gather(r, what):
-        @pl.when(along(r) != 0)
+        return chip_decay[k] * state + p1[k].astype(F32)
+
+    def zg(b):
+        return pltpu.make_async_remote_copy(
+            pre.at[b % HZ], c2.at[piece_at], zg_s.at[b % HZ], zg_r.at[mine_k],
+            device_id=chip(b), device_id_type=MESH,
+        )
+
+    def zg_from(k):
+        rows = pl.ds(k * STATE_PIECE, STATE_PIECE)
+        return pltpu.make_async_remote_copy(
+            pre.at[0], c2.at[rows], zg_s.at[0], zg_r.at[k], device_id=peer, device_id_type=MESH
+        )
+
+    def give(b):
+        @pl.when(z != b)
         def _():
-            what(zg(r))
-
-    @pl.when(lower)
-    def _():
+            zg(b).start()
+
+    def given(blocks):
+        for b in blocks:
+            @pl.when(z != b)
+            def _(b=b):
+                zg(b).wait_send()
+
+    def early():
+        return pltpu.make_async_remote_copy(
+            pre.at[EARLY], p1.at[EARLY - 1], zs_s.at[0], zs_r.at[EARLY - 1],
+            device_id=chip(NZ - 1 - z), device_id_type=MESH,
+        )
+
+    @pl.when(jnp.logical_and(owns, lower))
+    def _():
+        p1[z] = tot[piece_at, :]
+        decays(0, HZ - 1)
+        state = jnp.zeros((STATE_PIECE, HD), F32)
         for k in range(HZ - 1):
             arrive(k)
-
-        @pl.when(z < HZ - 1)
-        def _():
-            dz_from(HZ - 1).wait_recv()
-
-        state = jnp.zeros((STATE_PIECE, HD), F32)
-        for k in range(HZ - 1):
-            pre[k] = state.astype(BF16)
             state = advance(state, k)
-        pre[HZ - 1] = state.astype(BF16)
-
-    @pl.when(jnp.logical_not(lower))
-    def _():
-        for k in range(NZ - 1):
+            pre[k + 1] = state.astype(BF16)
+            give(k + 1)
+            if k == EARLY - 1:
+                @pl.when(jnp.logical_not(far))
+                def _():
+                    pl.semaphore_wait(far_sem, HZ)
+
+                early().start()
+
+    @pl.when(jnp.logical_and(owns, jnp.logical_not(lower)))
+    def _():
+        p1[z] = tot[piece_at, :]
+        decays(EARLY, NZ - 1)
+        zs_from(EARLY - 1).wait_recv()
+        state = p1[EARLY - 1].astype(F32)
+        for k in range(EARLY, NZ - 1):
             arrive(k)
-
-        @pl.when(z < NZ - 1)
-        def _():
-            dz_from(NZ - 1).wait_recv()
-
-        state = jnp.zeros((STATE_PIECE, HD), F32)
-        for k in range(NZ - 1):
-            if k >= HZ:
-                pre[k - HZ] = state.astype(BF16)
             state = advance(state, k)
-        pre[HZ - 1] = state.astype(BF16)
-
-    for r in ZH:
-        gather(r, lambda copy: copy.start())
-    c2[piece_at, :] = pre[zh]
-    lax.fori_loop(HEADS // 2, HEADS, attend, 0)
+            if k >= HZ - 1:
+                pre[k + 1 - HZ] = state.astype(BF16)
+        for b in (15, 8, 14, 9, 13, 12, 10, 11):
+            give(b)
+
+    @pl.when(owns)
+    def _():
+        c2[piece_at, :] = pre[zh]
+
+    lax.fori_loop(blocks_before, HALF // BLK, queries, 0)
+    lax.fori_loop(heads_before, HEADS, attend, 0)
     for r in XY:
         ag(r).wait_send()
 
-    @pl.when(zh < HZ - 1)
-    def _():
-        for r in ZH:
-            zs(along(r), r).wait_send()
-
-    @pl.when(lower)
-    def _():
-        for r in range(HZ):
-            dz(HZ + lax.rem(z + r, HZ), HZ + r).wait_send()
-            zs(HZ + lax.rem(z + r, HZ), HZ + r).wait_send()
+    @pl.when(adds)
+    def _():
+        to_owners(base_z, lambda owner, k: zs(owner, k).wait_send())
+
+    @pl.when(far)
+    def _():
+        def sent(owner, k):
+            dz(owner).wait_send()
+            zs(owner, k).wait_send()
+
+        to_far(sent)
 
     @pl.when(z != 0)
     def _():
-        for r in ZH:
-            zg(r).wait_recv()
+        to_owners(base_z, lambda owner, k: zg_from(k).wait_recv())
 
     @pl.when(z == 0)
     def _():
@@ -433,14 +501,7 @@
     )
     swap_carried.start()
 
-    def write(pair, b, slot):
-        rows = pl.ds(b * BLK, BLK)
-        lanes = pl.ds(pl.multiple_of(pair * PAIR, PAIR), PAIR)
-        return pltpu.make_async_copy(
-            out_v.at[rows, lanes], out_hbm.at[rows, lanes], out_sem.at[slot]
-        )
-
-    def finish(pair, slot):
+    def finish(pair):
         for b in range(TOK // BLK):
             rows = pl.ds(b * BLK, BLK)
             for e in range(2):
@@ -452,23 +513,23 @@
                 out_v[rows, at] = (
                     att * lax.rsqrt(square + 1e-6) * gain[pl.ds(pair * 2 + e, 1), :]
                 ).astype(BF16)
-            write(pair, b, slot * 4 + b).start()
-
-    finish(c, 0)
+
+    finish(c)
     swap_carried.wait()
     for e in range(2):
         at = pl.ds(pl.multiple_of((1 - c) * PAIR + e * HD, HD), HD)
         decay = jnp.exp(dl_own[pl.ds((1 - c) * 2 + e, 1), :])
         st_v[at, :] = decay * carried[at, :].astype(F32) + loc[at, :]
-    store_state = pltpu.make_async_copy(st_v, st_hbm, st_sem)
-    store_state.start()
-    finish(1 - c, 1)
-    for r in ZH:
-        gather(r, lambda copy: copy.wait_send())
-    for b in range(TOK // BLK):
-        write(c, b, b).wait()
-        write(1 - c, b, 4 + b).wait()
-    store_state.wait()
+    finish(1 - c)
+
+    @pl.when(jnp.logical_and(owns, lower))
+    def _():
+        given(range(1, HZ))
+        early().wait_send()
+
+    @pl.when(jnp.logical_and(owns, jnp.logical_not(lower)))
+    def _():
+        given(range(HZ, NZ))
 
 
 def local(hidden, base, down, up, decay, gain):
@@ -489,13 +550,13 @@
         pltpu.VMEM((HEADS, TOK, HD), F32),
         pltpu.VMEM((8, HD), F32),
         pltpu.VMEM((8, HD), F32),
-        pltpu.VMEM((NZ, 8, HD), F32),
+        pltpu.VMEM((NZ, 1, HD), F32),
+        pltpu.VMEM((NZ, 1, HD), F32),
         pltpu.VMEM((TOK, WIDTH), BF16),
         pltpu.VMEM((TOK, WIDTH), BF16),
         pltpu.VMEM((WIDTH, TOK), BF16),
         pltpu.VMEM((TOK, WIDTH), BF16),
         pltpu.VMEM((TOK, WIDTH), F32),
-        pltpu.VMEM((TOK, WIDTH), BF16),
         pltpu.VMEM((WIDTH, HD), F32),
         pltpu.VMEM((PAIR, HD), BF16),
         pltpu.VMEM((PAIR, HD), BF16),
@@ -504,8 +565,7 @@
         pltpu.VMEM((HZ, STATE_PIECE, HD), BF16),
         pltpu.VMEM((PAIR, HD), BF16),
         pltpu.VMEM((WIDTH, HD), BF16),
-        pltpu.VMEM((WIDTH, HD), F32),
-        dma((6,)), dma((8,)), dma,
+        dma((6,)),
         dma((NTP,)), dma((NTP,)), dma((NTP,)), dma((NTP,)),
         dma((NZ,)), dma((NZ,)), dma((NZ,)), dma((NZ,)), dma((NZ,)), dma((NZ,)),
         dma((3,)), dma((3,)), pltpu.SemaphoreType.REGULAR, pltpu.SemaphoreType.REGULAR,
@@ -517,7 +577,7 @@
             jax.ShapeDtypeStruct((WIDTH, HD), F32),
         ),
         in_specs=[anyspace] * 6,
-        out_specs=(anyspace, anyspace),
+        out_specs=(pl.BlockSpec(memory_space=pltpu.VMEM),) * 2,
         scratch_shapes=scratch,
         compiler_params=pltpu.CompilerParams(
             collective_id=0, has_side_effects=True, vmem_limit_bytes=48 * 1024 * 1024

time: 43.8 us -> 40 us (0.913)
  the two profiles are of different devices: /device:TPU:257 before, /device:TPU:481 now
where the time goes in v3:
time: 40 us; the launch traced here: 39.9 us
  Pallas kernels  37.6 us (94%)
  local copies, waits for them, and re-layouts  1.67 us (4%)
  between operations  0.64 us (2%)
    pallas_call x1, Pallas kernels, local(): pl.pallas_call(kernel, out_shape=(jax.ShapeDtypeStruct((TOK, WIDTH), BF16...  37.6 us
    unnamed x2, local copies, waits for them, and re-layouts  1.67 us

profile of v3, /device:TPU:481, one launch (start us, length us, event | category | flops | bytes accessed | tf_op | source)
XLA Modules:
  0.0 39.9 jit_solution(16064951562632323190)
XLA Ops:
  0.6 37.6 %shard_map.77 = (bf16[1024,512]{1,0:T(8,128)(2,1)S(1)}, f32[512,128]{1,0:T(8,128)S(1)}) custom-call(bf16[1024,384]{1,0:T(8,128)(2,1)} %hid_hbm.1, bf16[3,1024,512]{2,1,0:T(8,128)(2,1)} %base_hbm.1, bf16[64,384]{1,0:T(8,128)(2,1)} %bitcast.5, bf16[3,64,512]{2,1,0:T(8,128)(2,1)} %up_hbm.1, f32[4,1024]{1,0:T(4,128)} %bitcast.6, f32[4,128]{1,0:T(4,128)} %bitcast.7), custom_call_target="tpu_custom_call" | custom-call | flops 3000000000 | bytes 6000000 | tf_op jit(solution)/shard_map/pallas_call | solution.py:573
  38.2 1.0 %copy.10 = bf16[1024,512]{1,0:T(8,128)(2,1)} copy(bf16[1024,512]{1,0:T(8,128)(2,1)S(1)} %get-tuple-element.8) | data formatting | bytes 2097152
  39.2 0.7 %copy.11 = f32[1,4,128,128]{3,2,1,0:T(8,128)} copy(f32[1,4,128,128]{3,2,1,0:T(8,128)S(1)} %bitcast.4) | data formatting | bytes 524288

commit v4 on v3

--- a/solution.py
+++ b/solution.py
@@ -21,7 +21,7 @@
 HZ = NZ // 2
 OWNERS = 4
 FIRST = 2
-EARLY = 5
+EARLY = 7
 STATE_PIECE = PAIR // OWNERS
 LANES = HD // HEADS
 MESH = pl.DeviceIdType.MESH
@@ -40,6 +40,7 @@
     return jnp.where(z < HZ, z, jnp.where(z >= 12, 23 - z, z + 4))
 
 
+CROSS = [*range(FIRST, FIRST + OWNERS), *range(max(EARLY, FIRST + OWNERS), HZ)]
 ORDER = [z if z < HZ else (23 - z if z >= 12 else z + 4) for z in range(NZ)]
 
 
@@ -138,7 +139,7 @@
         def _(k=k):
             pl.semaphore_signal(near_sem, inc=1, device_id=chip(k), device_id_type=MESH)
 
-        @pl.when(jnp.logical_and(place > ORDER[k], jnp.logical_and(jnp.logical_not(same), k >= FIRST)))
+        @pl.when(jnp.logical_and(place > ORDER[k], jnp.logical_and(jnp.logical_not(same), k in CROSS)))
         def _(k=k):
             pl.semaphore_signal(far_sem, inc=1, device_id=chip(k), device_id_type=MESH)
 
@@ -218,7 +219,7 @@
     def _():
         pl.semaphore_wait(near_sem, later)
 
-    adds = zh < HZ - 1
+    adds = jnp.logical_or(zh < HZ - 1, jnp.logical_and(lower, EARLY == HZ))
 
     @pl.when(adds)
     def _():
@@ -310,6 +311,15 @@
     def _():
         to_owners(base_z, lambda owner, k: zs(owner, k).start())
 
+    def first():
+        return pltpu.make_async_remote_copy(
+            tot, c2, core_s.at[3], core_r.at[3], device_id=chip(1), device_id_type=MESH
+        )
+
+    @pl.when(z == 0)
+    def _():
+        first().start()
+
     far = jnp.logical_and(lower, z >= EARLY)
 
     def to_far(what):
@@ -367,10 +377,8 @@
             inside[rows, at] = acc
         return carry
 
-    scan_first = jnp.logical_or(z == 4, z == 5)
-    blocks_before = jnp.where(scan_first, 0, HALF // BLK)
-    heads_before = jnp.where(scan_first, 0, HEADS // 2)
-    lax.fori_loop(0, blocks_before, queries, 0)
+    heads_before = jnp.where(jnp.logical_or(z == 4, z == 5), 1, 2)
+    lax.fori_loop(0, HALF // BLK, queries, 0)
     lax.fori_loop(0, heads_before, attend, 0)
 
     head_lane = (c * 2 + mine_k // 2) * LANES
@@ -420,26 +428,28 @@
 
     def early():
         return pltpu.make_async_remote_copy(
-            pre.at[EARLY], p1.at[EARLY - 1], zs_s.at[0], zs_r.at[EARLY - 1],
+            pre.at[EARLY % HZ], p1.at[EARLY - 1], zs_s.at[0], zs_r.at[EARLY - 1],
             device_id=chip(NZ - 1 - z), device_id_type=MESH,
         )
 
     @pl.when(jnp.logical_and(owns, lower))
     def _():
         p1[z] = tot[piece_at, :]
-        decays(0, HZ - 1)
+        ends = max(HZ - 1, EARLY)
+        decays(0, ends)
         state = jnp.zeros((STATE_PIECE, HD), F32)
-        for k in range(HZ - 1):
+        for k in range(ends):
             arrive(k)
             state = advance(state, k)
-            pre[k + 1] = state.astype(BF16)
-            give(k + 1)
+            pre[(k + 1) % HZ] = state.astype(BF16)
             if k == EARLY - 1:
                 @pl.when(jnp.logical_not(far))
                 def _():
                     pl.semaphore_wait(far_sem, HZ)
 
                 early().start()
+            if 1 < k + 1 < HZ:
+                give(k + 1)
 
     @pl.when(jnp.logical_and(owns, jnp.logical_not(lower)))
     def _():
@@ -459,7 +469,6 @@
     def _():
         c2[piece_at, :] = pre[zh]
 
-    lax.fori_loop(blocks_before, HALF // BLK, queries, 0)
     lax.fori_loop(heads_before, HEADS, attend, 0)
     for r in XY:
         ag(r).wait_send()
@@ -476,12 +485,17 @@
 
         to_far(sent)
 
-    @pl.when(z != 0)
+    @pl.when(z > 1)
     def _():
         to_owners(base_z, lambda owner, k: zg_from(k).wait_recv())
 
+    @pl.when(z == 1)
+    def _():
+        first().wait_recv()
+
     @pl.when(z == 0)
     def _():
+        first().wait_send()
         c2[...] = jnp.zeros_like(c2)
 
     for e in range(2):
@@ -524,7 +538,7 @@
 
     @pl.when(jnp.logical_and(owns, lower))
     def _():
-        given(range(1, HZ))
+        given(range(2, HZ))
         early().wait_send()
 
     @pl.when(jnp.logical_and(owns, jnp.logical_not(lower)))
@@ -568,7 +582,7 @@
         dma((6,)),
         dma((NTP,)), dma((NTP,)), dma((NTP,)), dma((NTP,)),
         dma((NZ,)), dma((NZ,)), dma((NZ,)), dma((NZ,)), dma((NZ,)), dma((NZ,)),
-        dma((3,)), dma((3,)), pltpu.SemaphoreType.REGULAR, pltpu.SemaphoreType.REGULAR,
+        dma((4,)), dma((4,)), pltpu.SemaphoreType.REGULAR, pltpu.SemaphoreType.REGULAR,
     ]
     mixed, states = pl.pallas_call(
         kernel,

time: 40 us -> 38 us (0.950)
  Pallas kernels: 37.6 us -> 35.5 us
    pallas_call x1, Pallas kernels: 37.6 us -> 35.5 us  [local(): pl.pallas_call(kernel, out_shape=(jax.ShapeDtypeStruct((TOK, WIDTH), BF16...]
where the time goes in v4:
time: 38 us; the launch traced here: 37.9 us
  Pallas kernels  35.5 us (93%)
  local copies, waits for them, and re-layouts  1.67 us (4%)
  between operations  0.64 us (2%)
    pallas_call x1, Pallas kernels, local(): pl.pallas_call(kernel, out_shape=(jax.ShapeDtypeStruct((TOK, WIDTH), BF16...  35.5 us
    unnamed x2, local copies, waits for them, and re-layouts  1.67 us

profile of v4, /device:TPU:481, one launch (start us, length us, event | category | flops | bytes accessed | tf_op | source)
XLA Modules:
  0.0 37.9 jit_solution(1734522187439616388)
XLA Ops:
  0.6 35.5 %shard_map.77 = (bf16[1024,512]{1,0:T(8,128)(2,1)S(1)}, f32[512,128]{1,0:T(8,128)S(1)}) custom-call(bf16[1024,384]{1,0:T(8,128)(2,1)} %hid_hbm.1, bf16[3,1024,512]{2,1,0:T(8,128)(2,1)} %base_hbm.1, bf16[64,384]{1,0:T(8,128)(2,1)} %bitcast.5, bf16[3,64,512]{2,1,0:T(8,128)(2,1)} %up_hbm.1, f32[4,1024]{1,0:T(4,128)} %bitcast.6, f32[4,128]{1,0:T(4,128)} %bitcast.7), custom_call_target="tpu_custom_call" | custom-call | flops 3000000000 | bytes 6000000 | tf_op jit(solution)/shard_map/pallas_call | solution.py:587
  36.2 1.0 %copy.10 = bf16[1024,512]{1,0:T(8,128)(2,1)} copy(bf16[1024,512]{1,0:T(8,128)(2,1)S(1)} %get-tuple-element.8) | data formatting | bytes 2097152
  37.2 0.7 %copy.11 = f32[1,4,128,128]{3,2,1,0:T(8,128)} copy(f32[1,4,128,128]{3,2,1,0:T(8,128)S(1)} %bitcast.4) | data formatting | bytes 524288

commit v5 on v4

--- a/solution.py
+++ b/solution.py
@@ -52,7 +52,7 @@
 def kernel(
     hid_hbm, base_hbm, dwn_hbm, up_hbm, dec_hbm, gain_hbm,
     out_v, st_v,
-    hid, base, dpad, upad, dec, gain,
+    hid, base, dpad, upad, dec, gain, kbase, kup,
     part, rsum, lora,
     cum, wgt, ccol, dl_own, dl_peer, dl_chip, chip_decay,
     q_ref, qs_ref, kt_ref, v_ref, inside,
@@ -78,16 +78,6 @@
     def along(r):
         return base_z + lax.rem(zh + r, HZ)
 
-    place = order(z)
-    barrier = pltpu.get_barrier_semaphore()
-    for r in XY:
-        pl.semaphore_signal(barrier, inc=1, device_id=plane(r), device_id_type=MESH)
-    pl.semaphore_signal(barrier, inc=1, device_id=peer, device_id_type=MESH)
-    for k in range(NZ):
-        @pl.when(place < ORDER[k])
-        def _(k=k):
-            pl.semaphore_signal(barrier, inc=1, device_id=chip(k), device_id_type=MESH)
-
     loads = [
         pltpu.make_async_copy(dwn_hbm, dpad.at[pl.ds(RANK, RANK)], in_sem.at[0]),
         pltpu.make_async_copy(hid_hbm, hid, in_sem.at[1]),
@@ -96,8 +86,20 @@
         pltpu.make_async_copy(base_hbm, base, in_sem.at[4]),
         pltpu.make_async_copy(gain_hbm, gain, in_sem.at[5]),
     ]
-    for load in loads:
+    loads[0].start()
+    loads[1].start()
+
+    place = order(z)
+    barrier = pltpu.get_barrier_semaphore()
+    for r in XY:
+        pl.semaphore_signal(barrier, inc=1, device_id=plane(r), device_id_type=MESH)
+    pl.semaphore_signal(barrier, inc=1, device_id=peer, device_id_type=MESH)
+    for load in loads[2:]:
         load.start()
+    for k in range(NZ):
+        @pl.when(place < ORDER[k])
+        def _(k=k):
+            pl.semaphore_signal(barrier, inc=1, device_id=chip(k), device_id_type=MESH)
 
     zeros = jnp.zeros((RANK, GROUP), BF16)
     dpad[pl.ds(0, RANK), :] = zeros
@@ -159,11 +161,17 @@
     )
     swap_decay.start()
 
-    def ccol_of(h, carry):
-        ccol[h] = jnp.broadcast_to(cum[pl.ds(h, 1), :], (HD, TOK)).T
+    loads[3].wait()
+    loads[4].wait()
+
+    def turn(i, carry):
+        at = pl.ds(pl.multiple_of(i * BLK, BLK), BLK)
+        kbase[:, at] = base[1, at, :].T
         return carry
 
-    lax.fori_loop(0, HEADS, ccol_of, 0)
+    lax.fori_loop(0, TOK // BLK, turn, 0)
+    kup[0] = upad[1, pl.ds(RANK, 2 * RANK), :].T
+    kup[1] = upad[1, pl.ds(0, 2 * RANK), :].T
 
     swap_decay.wait()
     head_of_lane = lax.broadcasted_iota(jnp.int32, (8, HD), 1) // LANES
@@ -225,8 +233,6 @@
     def _():
         to_owners(base_z, lambda owner, k: dz(owner).start())
 
-    loads[3].wait()
-    loads[4].wait()
     loads[5].wait()
 
     def projected(i, a, row, size, lanes):
@@ -244,7 +250,12 @@
         scaled = []
         for a in range(2):
             at = pl.ds(pl.multiple_of(a * HALF + row, CHUNK), CHUNK)
-            k = silu(projected(1, a, row, CHUNK, slice(None))).astype(BF16).T
+            k = silu(
+                kbase[:, at].astype(F32)
+                + lax.dot_general(
+                    kup[a], lora[pl.ds(row, CHUNK), :], trans_b, preferred_element_type=F32
+                )
+            ).astype(BF16)
             kt_ref[:, at] = k
             v_ref[at, :] = projected(2, a, row, CHUNK, slice(None)).astype(BF16)
             scaled.append(
@@ -277,11 +288,7 @@
         loc_send, loc_recv, core_s.at[1], core_r.at[1], device_id=peer, device_id_type=MESH
     )
     swap_local.start()
-    @pl.when(adds)
-    def _():
-        to_owners(base_z, lambda owner, k: dz(owner).wait_send())
-
-    swap_local.wait()
+    swap_local.wait_recv()
 
     def per_row(ref, e):
         return jnp.exp(ref[pl.ds(c * 2 + e, 1), :])
@@ -378,6 +385,11 @@
         return carry
 
     heads_before = jnp.where(jnp.logical_or(z == 4, z == 5), 1, 2)
+    def ccol_of(h, carry):
+        ccol[h] = jnp.broadcast_to(cum[pl.ds(h, 1), :], (HD, TOK)).T
+        return carry
+
+    lax.fori_loop(0, HEADS, ccol_of, 0)
     lax.fori_loop(0, HALF // BLK, queries, 0)
     lax.fori_loop(0, heads_before, attend, 0)
 
@@ -473,8 +485,11 @@
     for r in XY:
         ag(r).wait_send()
 
+    swap_local.wait_send()
+
     @pl.when(adds)
     def _():
+        to_owners(base_z, lambda owner, k: dz(owner).wait_send())
         to_owners(base_z, lambda owner, k: zs(owner, k).wait_send())
 
     @pl.when(far)
@@ -498,22 +513,24 @@
         first().wait_send()
         c2[...] = jnp.zeros_like(c2)
 
+    states = []
     for e in range(2):
         rows = pl.ds(e * HD, HD)
-        at = pl.ds(pl.multiple_of(c * PAIR + e * HD, HD), HD)
-        own = loc[at, :]
+        own = loc[pl.ds(pl.multiple_of(c * PAIR + e * HD, HD), HD), :]
         before = c2[rows, :].astype(F32)
         even_decay = jnp.where(even, per_row(dl_own, e), per_row(dl_peer, e))
         after = even_decay * before + jnp.where(even, own, loc_recv[rows, :].astype(F32))
         loc_send[rows, :] = jnp.where(even, after, before).astype(BF16)
-        here = jnp.where(even, before, after)
-        carried[at, :] = here.astype(BF16)
-        st_v[at, :] = per_row(dl_own, e) * here + own
+        states.append((own, jnp.where(even, before, after)))
     swap_carried = pltpu.make_async_remote_copy(
         loc_send, carried.at[ours], core_s.at[2], core_r.at[2],
         device_id=peer, device_id_type=MESH,
     )
     swap_carried.start()
+    for e, (own, here) in enumerate(states):
+        at = pl.ds(pl.multiple_of(c * PAIR + e * HD, HD), HD)
+        carried[at, :] = here.astype(BF16)
+        st_v[at, :] = per_row(dl_own, e) * here + own
 
     def finish(pair):
         for b in range(TOK // BLK):
@@ -529,12 +546,14 @@
                 ).astype(BF16)
 
     finish(c)
-    swap_carried.wait()
+    swap_carried.wait_recv()
     for e in range(2):
         at = pl.ds(pl.multiple_of((1 - c) * PAIR + e * HD, HD), HD)
         decay = jnp.exp(dl_own[pl.ds((1 - c) * 2 + e, 1), :])
         st_v[at, :] = decay * carried[at, :].astype(F32) + loc[at, :]
     finish(1 - c)
+
+    swap_carried.wait_send()
 
     @pl.when(jnp.logical_and(owns, lower))
     def _():
@@ -556,6 +575,8 @@
         pltpu.VMEM((3, 3 * RANK, WIDTH), BF16),
         pltpu.VMEM((HEADS, TOK), F32),
         pltpu.VMEM((HEADS, HD), F32),
+        pltpu.VMEM((WIDTH, TOK), BF16),
+        pltpu.VMEM((2, WIDTH, 2 * RANK), BF16),
         pltpu.VMEM((HALF, 2 * RANK), BF16),
         pltpu.VMEM((NTP, LORA_PIECE, 2 * RANK), BF16),
         pltpu.VMEM((HALF, 2 * RANK), BF16),

time: 38 us -> 37.4 us (0.984)
  Pallas kernels: 35.5 us -> 35 us
    pallas_call x1, Pallas kernels: 35.5 us -> 35 us  [local(): pl.pallas_call(kernel, out_shape=(jax.ShapeDtypeStruct((TOK, WIDTH), BF16...]
where the time goes in v5:
time: 37.4 us; the launch traced here: 37.3 us
  Pallas kernels  35 us (94%)
  local copies, waits for them, and re-layouts  1.67 us (4%)
  between operations  0.64 us (2%)
    pallas_call x1, Pallas kernels, local(): pl.pallas_call(kernel, out_shape=(jax.ShapeDtypeStruct((TOK, WIDTH), BF16...  35 us
    unnamed x2, local copies, waits for them, and re-layouts  1.67 us

profile of v5, /device:TPU:481, one launch (start us, length us, event | category | flops | bytes accessed | tf_op | source)
XLA Modules:
  0.0 37.3 jit_solution(12258441001350692100)
XLA Ops:
  0.6 35.0 %shard_map.77 = (bf16[1024,512]{1,0:T(8,128)(2,1)S(1)}, f32[512,128]{1,0:T(8,128)S(1)}) custom-call(bf16[1024,384]{1,0:T(8,128)(2,1)} %hid_hbm.1, bf16[3,1024,512]{2,1,0:T(8,128)(2,1)} %base_hbm.1, bf16[64,384]{1,0:T(8,128)(2,1)} %bitcast.5, bf16[3,64,512]{2,1,0:T(8,128)(2,1)} %up_hbm.1, f32[4,1024]{1,0:T(4,128)} %bitcast.6, f32[4,128]{1,0:T(4,128)} %bitcast.7), custom_call_target="tpu_custom_call" | custom-call | flops 3000000000 | bytes 6000000 | tf_op jit(solution)/shard_map/pallas_call | solution.py:608
  35.6 1.0 %copy.10 = bf16[1024,512]{1,0:T(8,128)(2,1)} copy(bf16[1024,512]{1,0:T(8,128)(2,1)S(1)} %get-tuple-element.8) | data formatting | bytes 2097152
  36.6 0.7 %copy.11 = f32[1,4,128,128]{3,2,1,0:T(8,128)} copy(f32[1,4,128,128]{3,2,1,0:T(8,128)S(1)} %bitcast.4) | data formatting | bytes 524288

commit v6 on v5

--- a/solution.py
+++ b/solution.py
@@ -20,7 +20,8 @@
 CHUNK = HALF // NX
 HZ = NZ // 2
 OWNERS = 4
-FIRST = 2
+LOWER = (2, 3, 4, 5)
+UPPER = (13, 12, 10, 9)
 EARLY = 7
 STATE_PIECE = PAIR // OWNERS
 LANES = HD // HEADS
@@ -40,7 +41,7 @@
     return jnp.where(z < HZ, z, jnp.where(z >= 12, 23 - z, z + 4))
 
 
-CROSS = [*range(FIRST, FIRST + OWNERS), *range(max(EARLY, FIRST + OWNERS), HZ)]
+CROSS = sorted({*LOWER, *range(EARLY, HZ)})
 ORDER = [z if z < HZ else (23 - z if z >= 12 else z + 4) for z in range(NZ)]
 
 
@@ -56,7 +57,7 @@
     part, rsum, lora,
     cum, wgt, ccol, dl_own, dl_peer, dl_chip, chip_decay,
     q_ref, qs_ref, kt_ref, v_ref, inside,
-    loc, loc_send, loc_recv, tot, p1, pre, c2, carried,
+    loc, loc_send, loc_recv, tot, p1, pre, later_part, c2, carried,
     in_sem,
     rs_s, rs_r, ag_s, ag_r, zs_s, zs_r, zg_s, zg_r, dz_s, dz_r, core_s, core_r, near_sem, far_sem,
 ):
@@ -195,9 +196,9 @@
             device_id=peer, device_id_type=MESH,
         )
 
-    def to_owners(half, what):
+    def to_owners(what):
         for k in range(OWNERS):
-            owner = half + FIRST + jnp.where(lower, k, OWNERS - 1 - k)
+            owner = jnp.where(lower, LOWER[k], UPPER[k])
 
             @pl.when(owner != z)
             def _(owner=owner, k=k):
@@ -231,7 +232,7 @@
 
     @pl.when(adds)
     def _():
-        to_owners(base_z, lambda owner, k: dz(owner).start())
+        to_owners(lambda owner, k: dz(owner).start())
 
     loads[5].wait()
 
@@ -316,7 +317,7 @@
 
     @pl.when(adds)
     def _():
-        to_owners(base_z, lambda owner, k: zs(owner, k).start())
+        to_owners(lambda owner, k: zs(owner, k).start())
 
     def first():
         return pltpu.make_async_remote_copy(
@@ -331,7 +332,7 @@
 
     def to_far(what):
         for k in range(OWNERS):
-            what(HZ + FIRST + OWNERS - 1 - k, k)
+            what(UPPER[k], k)
 
     @pl.when(far)
     def _():
@@ -343,9 +344,12 @@
 
         to_far(start)
 
-    owns = jnp.logical_and(zh >= FIRST, zh < FIRST + OWNERS)
-    mine_k = jnp.where(lower, zh - FIRST, FIRST + OWNERS - 1 - zh)
-    mine_k = jnp.clip(mine_k, 0, OWNERS - 1)
+    mine_k, partner, owns = 0, 0, z < 0
+    for k in range(OWNERS):
+        here = jnp.logical_or(z == LOWER[k], z == UPPER[k])
+        mine_k = jnp.where(here, k, mine_k)
+        partner = jnp.where(here, UPPER[k], partner)
+        owns = jnp.logical_or(owns, here)
     piece_at = pl.ds(pl.multiple_of(mine_k * STATE_PIECE, STATE_PIECE), STATE_PIECE)
 
     def queries(i, carry):
@@ -384,7 +388,7 @@
             inside[rows, at] = acc
         return carry
 
-    heads_before = jnp.where(jnp.logical_or(z == 4, z == 5), 1, 2)
+    heads_before = jnp.where(z >= 4, 1, 2)
     def ccol_of(h, carry):
         ccol[h] = jnp.broadcast_to(cum[pl.ds(h, 1), :], (HD, TOK)).T
         return carry
@@ -441,7 +445,7 @@
     def early():
         return pltpu.make_async_remote_copy(
             pre.at[EARLY % HZ], p1.at[EARLY - 1], zs_s.at[0], zs_r.at[EARLY - 1],
-            device_id=chip(NZ - 1 - z), device_id_type=MESH,
+            device_id=chip(partner), device_id_type=MESH,
         )
 
     @pl.when(jnp.logical_and(owns, lower))
@@ -467,14 +471,20 @@
     def _():
         p1[z] = tot[piece_at, :]
         decays(EARLY, NZ - 1)
-        zs_from(EARLY - 1).wait_recv()
-        state = p1[EARLY - 1].astype(F32)
+        state = jnp.zeros((STATE_PIECE, HD), F32)
+        grow = jnp.ones((1, HD), F32)
+        grown = {}
         for k in range(EARLY, NZ - 1):
             arrive(k)
             state = advance(state, k)
+            grow = grow * chip_decay[k]
             if k >= HZ - 1:
-                pre[k + 1 - HZ] = state.astype(BF16)
+                later_part[k + 1 - HZ] = state
+                grown[k + 1] = grow
+        zs_from(EARLY - 1).wait_recv()
+        start = p1[EARLY - 1].astype(F32)
         for b in (15, 8, 14, 9, 13, 12, 10, 11):
+            pre[b - HZ] = (grown[b] * start + later_part[b - HZ]).astype(BF16)
             give(b)
 
     @pl.when(owns)
@@ -489,8 +499,8 @@
 
     @pl.when(adds)
     def _():
-        to_owners(base_z, lambda owner, k: dz(owner).wait_send())
-        to_owners(base_z, lambda owner, k: zs(owner, k).wait_send())
+        to_owners(lambda owner, k: dz(owner).wait_send())
+        to_owners(lambda owner, k: zs(owner, k).wait_send())
 
     @pl.when(far)
     def _():
@@ -502,7 +512,7 @@
 
     @pl.when(z > 1)
     def _():
-        to_owners(base_z, lambda owner, k: zg_from(k).wait_recv())
+        to_owners(lambda owner, k: zg_from(k).wait_recv())
 
     @pl.when(z == 1)
     def _():
@@ -532,7 +542,17 @@
         carried[at, :] = here.astype(BF16)
         st_v[at, :] = per_row(dl_own, e) * here + own
 
-    def finish(pair):
+    def finish(i, carry):
+        pair = jnp.where(i == 0, c, 1 - c)
+
+        @pl.when(i == 1)
+        def _():
+            swap_carried.wait_recv()
+            for e in range(2):
+                at = pl.ds(pl.multiple_of((1 - c) * PAIR + e * HD, HD), HD)
+                decay = jnp.exp(dl_own[pl.ds((1 - c) * 2 + e, 1), :])
+                st_v[at, :] = decay * carried[at, :].astype(F32) + loc[at, :]
+
         for b in range(TOK // BLK):
             rows = pl.ds(b * BLK, BLK)
             for e in range(2):
@@ -544,15 +564,9 @@
                 out_v[rows, at] = (
                     att * lax.rsqrt(square + 1e-6) * gain[pl.ds(pair * 2 + e, 1), :]
                 ).astype(BF16)
-
-    finish(c)
-    swap_carried.wait_recv()
-    for e in range(2):
-        at = pl.ds(pl.multiple_of((1 - c) * PAIR + e * HD, HD), HD)
-        decay = jnp.exp(dl_own[pl.ds((1 - c) * 2 + e, 1), :])
-        st_v[at, :] = decay * carried[at, :].astype(F32) + loc[at, :]
-    finish(1 - c)
-
+        return carry
+
+    lax.fori_loop(0, 2, finish, 0)
     swap_carried.wait_send()
 
     @pl.when(jnp.logical_and(owns, lower))
@@ -598,6 +612,7 @@
         pltpu.VMEM((PAIR, HD), BF16),
         pltpu.VMEM((NZ, STATE_PIECE, HD), BF16),
         pltpu.VMEM((HZ, STATE_PIECE, HD), BF16),
+        pltpu.VMEM((HZ, STATE_PIECE, HD), F32),
         pltpu.VMEM((PAIR, HD), BF16),
         pltpu.VMEM((WIDTH, HD), BF16),
         dma((6,)),

time: 37.4 us -> 37.1 us (level)
  Pallas kernels: 35 us -> 34.6 us
where the time goes in v6:
time: 37.1 us; the launch traced here: 37 us
  Pallas kernels  34.6 us (93%)
  local copies, waits for them, and re-layouts  1.67 us (5%)
  between operations  0.64 us (2%)
    pallas_call x1, Pallas kernels, local(): pl.pallas_call(kernel, out_shape=(jax.ShapeDtypeStruct((TOK, WIDTH), BF16...  34.6 us
    unnamed x2, local copies, waits for them, and re-layouts  1.67 us

profile of v6, /device:TPU:481, one launch (start us, length us, event | category | flops | bytes accessed | tf_op | source)
XLA Modules:
  0.0 37.0 jit_solution(12707894509250226743)
XLA Ops:
  0.6 34.6 %shard_map.77 = (bf16[1024,512]{1,0:T(8,128)(2,1)S(1)}, f32[512,128]{1,0:T(8,128)S(1)}) custom-call(bf16[1024,384]{1,0:T(8,128)(2,1)} %hid_hbm.1, bf16[3,1024,512]{2,1,0:T(8,128)(2,1)} %base_hbm.1, bf16[64,384]{1,0:T(8,128)(2,1)} %bitcast.5, bf16[3,64,512]{2,1,0:T(8,128)(2,1)} %up_hbm.1, f32[4,1024]{1,0:T(4,128)} %bitcast.6, f32[4,128]{1,0:T(4,128)} %bitcast.7), custom_call_target="tpu_custom_call" | custom-call | flops 3000000000 | bytes 6000000 | tf_op jit(solution)/shard_map/pallas_call | solution.py:623
  35.3 1.0 %copy.10 = bf16[1024,512]{1,0:T(8,128)(2,1)} copy(bf16[1024,512]{1,0:T(8,128)(2,1)S(1)} %get-tuple-element.8) | data formatting | bytes 2097152
  36.3 0.7 %copy.11 = f32[1,4,128,128]{3,2,1,0:T(8,128)} copy(f32[1,4,128,128]{3,2,1,0:T(8,128)S(1)} %bitcast.4) | data formatting | bytes 524288

commit v7 on v6

--- a/solution.py
+++ b/solution.py
@@ -510,10 +510,6 @@
 
         to_far(sent)
 
-    @pl.when(z > 1)
-    def _():
-        to_owners(lambda owner, k: zg_from(k).wait_recv())
-
     @pl.when(z == 1)
     def _():
         first().wait_recv()
@@ -523,20 +519,30 @@
         first().wait_send()
         c2[...] = jnp.zeros_like(c2)
 
+    def swap_carried(e):
+        return pltpu.make_async_remote_copy(
+            loc_send.at[pl.ds(e * HD, HD)],
+            carried.at[pl.ds(pl.multiple_of(c * PAIR + e * HD, HD), HD)],
+            core_s.at[2 + 2 * e], core_r.at[2 + 2 * e], device_id=peer, device_id_type=MESH,
+        )
+
     states = []
     for e in range(2):
+        @pl.when(z > 1)
+        def _(e=e):
+            for k in (2 * e, 2 * e + 1):
+                @pl.when(z != jnp.where(lower, LOWER[k], UPPER[k]))
+                def _(k=k):
+                    zg_from(k).wait_recv()
+
         rows = pl.ds(e * HD, HD)
         own = loc[pl.ds(pl.multiple_of(c * PAIR + e * HD, HD), HD), :]
         before = c2[rows, :].astype(F32)
         even_decay = jnp.where(even, per_row(dl_own, e), per_row(dl_peer, e))
         after = even_decay * before + jnp.where(even, own, loc_recv[rows, :].astype(F32))
         loc_send[rows, :] = jnp.where(even, after, before).astype(BF16)
+        swap_carried(e).start()
         states.append((own, jnp.where(even, before, after)))
-    swap_carried = pltpu.make_async_remote_copy(
-        loc_send, carried.at[ours], core_s.at[2], core_r.at[2],
-        device_id=peer, device_id_type=MESH,
-    )
-    swap_carried.start()
     for e, (own, here) in enumerate(states):
         at = pl.ds(pl.multiple_of(c * PAIR + e * HD, HD), HD)
         carried[at, :] = here.astype(BF16)
@@ -547,7 +553,8 @@
 
         @pl.when(i == 1)
         def _():
-            swap_carried.wait_recv()
+            for e in range(2):
+                swap_carried(e).wait_recv()
             for e in range(2):
                 at = pl.ds(pl.multiple_of((1 - c) * PAIR + e * HD, HD), HD)
                 decay = jnp.exp(dl_own[pl.ds((1 - c) * 2 + e, 1), :])
@@ -567,7 +574,8 @@
         return carry
 
     lax.fori_loop(0, 2, finish, 0)
-    swap_carried.wait_send()
+    for e in range(2):
+        swap_carried(e).wait_send()
 
     @pl.when(jnp.logical_and(owns, lower))
     def _():
@@ -618,7 +626,7 @@
         dma((6,)),
         dma((NTP,)), dma((NTP,)), dma((NTP,)), dma((NTP,)),
         dma((NZ,)), dma((NZ,)), dma((NZ,)), dma((NZ,)), dma((NZ,)), dma((NZ,)),
-        dma((4,)), dma((4,)), pltpu.SemaphoreType.REGULAR, pltpu.SemaphoreType.REGULAR,
+        dma((5,)), dma((5,)), pltpu.SemaphoreType.REGULAR, pltpu.SemaphoreType.REGULAR,
     ]
     mixed, states = pl.pallas_call(
         kernel,

time: 37.1 us -> 37.1 us (level)
  no operation moved by 1% of the time
where the time goes in v7:
time: 37.1 us; the launch traced here: 36.9 us
  Pallas kernels  34.6 us (93%)
  local copies, waits for them, and re-layouts  1.67 us (5%)
  between operations  0.64 us (2%)
    pallas_call x1, Pallas kernels, local(): pl.pallas_call(kernel, out_shape=(jax.ShapeDtypeStruct((TOK, WIDTH), BF16...  34.6 us
    unnamed x2, local copies, waits for them, and re-layouts  1.67 us

profile of v7, /device:TPU:481, one launch (start us, length us, event | category | flops | bytes accessed | tf_op | source)
XLA Modules:
  0.0 36.9 jit_solution(8609478439912327011)
XLA Ops:
  0.6 34.6 %shard_map.77 = (bf16[1024,512]{1,0:T(8,128)(2,1)S(1)}, f32[512,128]{1,0:T(8,128)S(1)}) custom-call(bf16[1024,384]{1,0:T(8,128)(2,1)} %hid_hbm.1, bf16[3,1024,512]{2,1,0:T(8,128)(2,1)} %base_hbm.1, bf16[64,384]{1,0:T(8,128)(2,1)} %bitcast.5, bf16[3,64,512]{2,1,0:T(8,128)(2,1)} %up_hbm.1, f32[4,1024]{1,0:T(4,128)} %bitcast.6, f32[4,128]{1,0:T(4,128)} %bitcast.7), custom_call_target="tpu_custom_call" | custom-call | flops 3000000000 | bytes 6000000 | tf_op jit(solution)/shard_map/pallas_call | solution.py:631
  35.2 1.0 %copy.10 = bf16[1024,512]{1,0:T(8,128)(2,1)} copy(bf16[1024,512]{1,0:T(8,128)(2,1)S(1)} %get-tuple-element.8) | data formatting | bytes 2097152
  36.2 0.7 %copy.11 = f32[1,4,128,128]{3,2,1,0:T(8,128)} copy(f32[1,4,128,128]{3,2,1,0:T(8,128)S(1)} %bitcast.4) | data formatting | bytes 524288
